TPU v7x, 32 devices: a whole 2x2x4 slice. The times are simulated.
32 devices in a mesh: pipe: 2 (over y), batch: 16 (over z, x, core).
Axes of the slice: x: 2, y: 2, z: 4, core: 2. Of those that a mesh axis runs over, the one named last changes fastest.
Arguments:
- inputs: bfloat16 [2, 8192, 768], P(None, 'batch'), may hold values from -6 to 6
- cotangent: bfloat16 [2, 8192, 768], P(None, 'batch'), may hold values from -6 to 6
- lengths: int32 [32], P('batch'), may hold values from 128 to 512, as said below
- assign: int32 [32], P('batch'), may hold values from 0 to 1, as said below
- query_key_value: bfloat16 [2, 768, 2304], P('pipe'), may hold values from -0.3125 to 0.3125
- out_weight: bfloat16 [2, 768, 768], P('pipe'), may hold values from -0.21875 to 0.21875
- up_weight: bfloat16 [2, 768, 3072], P('pipe'), may hold values from -0.21875 to 0.21875
- down_weight: bfloat16 [2, 3072, 768], P('pipe'), may hold values from -0.109375 to 0.109375
- model_gains: float32 [2, 3, 768], P('pipe'), may hold values from 0.5 to 1.5
- model_shifts: float32 [2, 7, 768], P('pipe'), may hold values from -2 to 2
- hidden_gains: float32 [2, 3072], P('pipe'), may hold values from 0.5 to 1.5
- hidden_shifts: float32 [2, 2, 3072], P('pipe'), may hold values from -2 to 2
Outputs:
- section_out: bfloat16 [2, 2, 8192, 768], P('pipe', None, 'batch')
- section_in_grad: bfloat16 [2, 2, 8192, 768], P('pipe', None, 'batch')
- query_key_value_grad: float32 [2, 768, 2304], P('pipe')
- out_weight_grad: float32 [2, 768, 768], P('pipe')
- up_weight_grad: float32 [2, 768, 3072], P('pipe')
- down_weight_grad: float32 [2, 3072, 768], P('pipe')
- model_gains_grad: float32 [2, 3, 768], P('pipe')
- model_shifts_grad: float32 [2, 7, 768], P('pipe')
- hidden_gains_grad: float32 [2, 3072], P('pipe')
- hidden_shifts_grad: float32 [2, 2, 3072], P('pipe')
Inputs may be any that keep to these rules, and one draw needn't show every extreme that they name: `lengths`: each device's 2 sequences fit a slot; one sequence of exactly 512 tokens in every draw. `assign`: each device's 2 entries name every micro-batch once.
All inputs are finite; a program needn't handle non-finite values.
Results may differ from a plain program's by a relative error of at most 0.025.
Values may be sent and summed in bfloat16 or wider, within the bound.
A program may use at most 384 MiB of HBM per device.

v0:
```python
import jax
import jax.numpy as jnp
from jax import lax
from jax.sharding import PartitionSpec as P

HEAD = 64


EPSILON = 1e-05
SCALE = 0.125


def passed_along(block, axis, distance):
    devices = range(lax.axis_size(axis))
    route = [(i - distance, i) for i in devices if i - distance in devices]
    return lax.ppermute(block, axis, route)


def normalize(values_in, gain, shift):
    centred = values_in - jnp.mean(values_in, axis=-1, keepdims=True)
    variance = jnp.mean(centred * centred, axis=-1, keepdims=True)
    return centred * lax.rsqrt(variance + EPSILON) * gain + shift


def gelu_exact(values_in):
    return 0.5 * values_in * (1.0 + lax.erf(values_in * 0.7071067811865476))


def visible_mask(start, block_rows, row_count, length):
    query_pos = start + jnp.arange(block_rows, dtype=jnp.int32)[:, None]
    key_pos = jnp.arange(row_count, dtype=jnp.int32)[None, :]
    return (key_pos <= query_pos) & ((key_pos < length) | (key_pos == query_pos))


def multiply(left, right):
    return jnp.dot(left, right, preferred_element_type=jnp.float32)


def multiply_left_t(left, right):
    return lax.dot_general(
        left, right, (((0,), (0,)), ((), ())), preferred_element_type=jnp.float32
    )


def multiply_right_t(left, right):
    return lax.dot_general(
        left, right, (((1,), (1,)), ((), ())), preferred_element_type=jnp.float32
    )


def attention_forward(queries, key_part, value_part, length):
    row_count = queries.shape[0]
    head_count = queries.shape[1] // HEAD
    block_rows = min(512, row_count)
    key_heads = key_part.reshape(row_count, head_count, HEAD)
    value_heads = value_part.reshape(row_count, head_count, HEAD)

    def one_block(start):
        query_block = queries.reshape(block_rows, head_count, HEAD)
        scores = (
            jnp.einsum("qhd,khd->hqk", query_block, key_heads, preferred_element_type=jnp.float32)
            * SCALE
        )
        allowed = visible_mask(start, block_rows, row_count, length)
        scores = jnp.where(allowed[None], scores, -1e30)
        row_max = jnp.max(scores, axis=-1, keepdims=True)
        exps = jnp.exp(scores - row_max)
        row_total = jnp.sum(exps, axis=-1, keepdims=True)
        probabilities = (exps / row_total).astype(jnp.bfloat16)
        attended = jnp.einsum(
            "hqk,khd->qhd", probabilities, value_heads, preferred_element_type=jnp.float32
        )
        return (
            attended.reshape(block_rows, head_count * HEAD),
            (row_max + jnp.log(row_total))[:, :, 0],
        )

    starts = jnp.arange(row_count // block_rows, dtype=jnp.int32) * block_rows
    attended, log_total = lax.map(one_block, starts)
    return (attended.reshape(row_count, head_count * HEAD), log_total)


def attention_backward(queries, key_part, value_part, log_total, grad_attended, length):
    row_count = queries.shape[0]
    head_count = queries.shape[1] // HEAD
    block_rows = min(512, row_count)
    query_heads = queries.reshape(row_count, head_count, HEAD)
    key_heads = key_part.reshape(row_count, head_count, HEAD)
    value_heads = value_part.reshape(row_count, head_count, HEAD)
    grad_heads = grad_attended.reshape(row_count, head_count, HEAD)

    def one_block(carry, block_items):
        key_sum, value_sum = carry
        start, total_block = block_items
        scores = (
            jnp.einsum("qhd,khd->hqk", query_heads, key_heads, preferred_element_type=jnp.float32)
            * SCALE
        )
        allowed = visible_mask(start, block_rows, row_count, length)[None]
        probabilities = jnp.where(allowed, jnp.exp(scores - total_block[:, :, None]), 0.0)
        d_probs = jnp.einsum(
            "qhd,khd->hqk", grad_heads, value_heads, preferred_element_type=jnp.float32
        )
        row_delta = jnp.sum(d_probs * probabilities, axis=-1, keepdims=True)
        d_scores = (probabilities * (d_probs - row_delta)).astype(jnp.bfloat16)
        d_query = (
            jnp.einsum("hqk,khd->qhd", d_scores, key_heads, preferred_element_type=jnp.float32)
            * SCALE
        )
        key_sum = (
            key_sum
            + jnp.einsum("hqk,qhd->khd", d_scores, query_heads, preferred_element_type=jnp.float32)
            * SCALE
        )
        value_sum = value_sum + jnp.einsum(
            "hqk,qhd->khd",
            probabilities.astype(jnp.bfloat16),
            grad_heads,
            preferred_element_type=jnp.float32,
        )
        return ((key_sum, value_sum), d_query.reshape(block_rows, head_count * HEAD))

    starts = jnp.arange(row_count // block_rows, dtype=jnp.int32) * block_rows
    zero_sum = jnp.zeros((row_count, head_count, HEAD), jnp.float32)
    (key_sum, value_sum), d_query = lax.scan(one_block, (zero_sum, zero_sum), (starts, log_total))
    model_width = head_count * HEAD
    return (
        d_query.reshape(row_count, model_width),
        key_sum.reshape(row_count, model_width),
        value_sum.reshape(row_count, model_width),
    )


def layer_forward(features, params, length):
    (
        qkv_weight,
        out_matrix,
        up_matrix,
        down_matrix,
        gains_model,
        shifts_model,
        gains_hidden,
        shifts_hidden,
    ) = params
    model_width = features.shape[1]
    normed_in = normalize(features, gains_model[0], shifts_model[0]).astype(jnp.bfloat16)
    input_bias = jnp.concatenate(
        [shifts_model[1], jnp.zeros_like(shifts_model[1]), shifts_model[2]]
    )
    projected = (multiply(normed_in, qkv_weight) + input_bias).astype(jnp.bfloat16)
    attended, log_total = attention_forward(
        projected[:, :model_width],
        projected[:, model_width : 2 * model_width],
        projected[:, 2 * model_width :],
        length,
    )
    normed_mix = normalize(attended, gains_model[1], shifts_model[3]).astype(jnp.bfloat16)
    residual = features + multiply(normed_mix, out_matrix) + shifts_model[4]
    normed_ffn = normalize(residual, gains_model[2], shifts_model[5]).astype(jnp.bfloat16)
    pre_act = multiply(normed_ffn, up_matrix) + shifts_hidden[0]
    normed_hidden = normalize(gelu_exact(pre_act), gains_hidden, shifts_hidden[1]).astype(
        jnp.bfloat16
    )
    output = residual + multiply(normed_hidden, down_matrix) + shifts_model[6]
    return (
        output,
        (
            features,
            normed_in,
            projected,
            log_total,
            attended,
            normed_mix,
            residual,
            normed_ffn,
            pre_act,
            normed_hidden,
        ),
    )


def layer_backward(grad_out, kept_state, params, length):
    (
        qkv_weight,
        out_matrix,
        up_matrix,
        down_matrix,
        gains_model,
        shifts_model,
        gains_hidden,
        shifts_hidden,
    ) = params
    (
        features,
        normed_in,
        projected,
        log_total,
        attended,
        normed_mix,
        residual,
        normed_ffn,
        pre_act,
        normed_hidden,
    ) = kept_state
    model_width = features.shape[1]
    d_down = grad_out.astype(jnp.bfloat16)
    down_grad = multiply_left_t(normed_hidden, d_down)
    down_bias_grad = jnp.sum(d_down.astype(jnp.float32), axis=0)
    d_hidden = multiply_right_t(d_down, down_matrix)
    activated, gelu_pullback = jax.vjp(gelu_exact, pre_act)
    unused, norm_pullback = jax.vjp(normalize, activated, gains_hidden, shifts_hidden[1])
    d_act, hidden_gain_grad, hidden_shift_grad = norm_pullback(d_hidden)
    (d_pre,) = gelu_pullback(d_act)
    d_pre = d_pre.astype(jnp.bfloat16)
    up_grad = multiply_left_t(normed_ffn, d_pre)
    up_bias_grad = jnp.sum(d_pre.astype(jnp.float32), axis=0)
    d_ffn = multiply_right_t(d_pre, up_matrix)
    unused, norm_pullback = jax.vjp(normalize, residual, gains_model[2], shifts_model[5])
    d_residual, ffn_gain_grad, ffn_shift_grad = norm_pullback(d_ffn)
    d_residual = d_residual + grad_out
    d_branch = d_residual.astype(jnp.bfloat16)
    out_grad = multiply_left_t(normed_mix, d_branch)
    out_bias_grad = jnp.sum(d_branch.astype(jnp.float32), axis=0)
    d_mix = multiply_right_t(d_branch, out_matrix)
    unused, norm_pullback = jax.vjp(normalize, attended, gains_model[1], shifts_model[3])
    d_attended, mix_gain_grad, mix_shift_grad = norm_pullback(d_mix)
    d_query, d_key, d_value = attention_backward(
        projected[:, :model_width],
        projected[:, model_width : 2 * model_width],
        projected[:, 2 * model_width :],
        log_total,
        d_attended.astype(jnp.bfloat16),
        length,
    )
    d_proj = jnp.concatenate([d_query, d_key, d_value], axis=1).astype(jnp.bfloat16)
    qkv_grad = multiply_left_t(normed_in, d_proj)
    proj_sums = jnp.sum(d_proj.astype(jnp.float32), axis=0)
    d_norm_in = multiply_right_t(d_proj, qkv_weight)
    unused, norm_pullback = jax.vjp(normalize, features, gains_model[0], shifts_model[0])
    d_features, in_gain_grad, in_shift_grad = norm_pullback(d_norm_in)
    d_features = d_features + d_residual
    gains_grad = jnp.stack([in_gain_grad, mix_gain_grad, ffn_gain_grad])
    shifts_grad = jnp.stack(
        [
            in_shift_grad,
            proj_sums[:model_width],
            proj_sums[2 * model_width :],
            mix_shift_grad,
            out_bias_grad,
            ffn_shift_grad,
            down_bias_grad,
        ]
    )
    hidden_grad = jnp.stack([up_bias_grad, hidden_shift_grad])
    return (
        d_features,
        (
            qkv_grad,
            out_grad,
            up_grad,
            down_grad,
            gains_grad,
            shifts_grad,
            hidden_gain_grad,
            hidden_grad,
        ),
    )


def put_slot(buffer, slot_index, usable, new_value):
    previous = lax.dynamic_index_in_dim(buffer, slot_index, 0, keepdims=False)
    return lax.dynamic_update_index_in_dim(
        buffer, jnp.where(usable, new_value, previous), slot_index, 0
    )


def shards(
    inputs,
    cotangent,
    lengths,
    assign,
    query_key_value,
    out_weight,
    up_weight,
    down_weight,
    model_gains,
    model_shifts,
    hidden_gains,
    hidden_shifts,
):
    section_count = lax.axis_size("pipe")
    pipe_rank = lax.axis_index("pipe")
    micro_count = inputs.shape[0]
    row_count = inputs.shape[1]
    model_width = inputs.shape[2]
    owners = assign[:, None] == jnp.arange(micro_count, dtype=jnp.int32)[None, :]
    slot_len = jnp.sum(jnp.where(owners, lengths[:, None], 0), axis=0)
    params = (
        query_key_value[0],
        out_weight[0],
        up_weight[0],
        down_weight[0],
        model_gains[0],
        model_shifts[0],
        hidden_gains[0],
        hidden_shifts[0],
    )
    positions = jnp.arange(row_count, dtype=jnp.int32)
    outputs = jnp.zeros((micro_count, row_count, model_width), jnp.bfloat16)
    stored = None
    outgoing = None
    for moment in range(micro_count + section_count - 1):
        slot_pos = moment - pipe_rank
        usable = (slot_pos >= 0) & (slot_pos < micro_count)
        slot_index = jnp.clip(slot_pos, 0, micro_count - 1)
        source = lax.dynamic_index_in_dim(inputs, slot_index, 0, keepdims=False)
        if moment > 0:
            arriving = passed_along(outgoing, "pipe", 1)
            source = jnp.where(pipe_rank == 0, source, arriving)
        result, kept_state = layer_forward(source.astype(jnp.float32), params, slot_len[slot_index])
        outgoing = result.astype(jnp.bfloat16)
        outputs = put_slot(outputs, slot_index, usable, outgoing)
        if stored is None:
            stored = tuple(
                (jnp.zeros((micro_count,) + item.shape, item.dtype) for item in kept_state)
            )
        stored = tuple(
            (put_slot(buffer, slot_index, usable, item) for buffer, item in zip(stored, kept_state))
        )
    in_grads = jnp.zeros((micro_count, row_count, model_width), jnp.bfloat16)
    totals = None
    shares = None
    returning = None
    for moment in range(micro_count + section_count - 1):
        slot_pos = moment - (section_count - 1 - pipe_rank)
        usable = (slot_pos >= 0) & (slot_pos < micro_count)
        slot_index = jnp.clip(slot_pos, 0, micro_count - 1)
        length = slot_len[slot_index]
        live_rows = (positions < length).astype(jnp.float32)[:, None]
        grad_out = (
            lax.dynamic_index_in_dim(cotangent, slot_index, 0, keepdims=False).astype(jnp.float32)
            * live_rows
        )
        if moment > 0:
            arriving = passed_along(returning, "pipe", -1)
            grad_out = jnp.where(
                pipe_rank == section_count - 1, grad_out, arriving.astype(jnp.float32)
            )
        kept_state = tuple(
            (lax.dynamic_index_in_dim(buffer, slot_index, 0, keepdims=False) for buffer in stored)
        )
        grad_in, gradients = layer_backward(grad_out, kept_state, params, length)
        returning = grad_in.astype(jnp.bfloat16)
        in_grads = put_slot(in_grads, slot_index, usable, returning)
        gradients = tuple((jnp.where(usable, item, 0.0) for item in gradients))
        totals = (
            gradients
            if totals is None
            else tuple((left + right for left, right in zip(totals, gradients)))
        )
    shares = (
        lax.psum_scatter(totals[0], "batch", scatter_dimension=1, tiled=True),
        lax.psum_scatter(totals[1], "batch", scatter_dimension=1, tiled=True),
        lax.psum_scatter(totals[2], "batch", scatter_dimension=1, tiled=True),
        lax.psum_scatter(totals[3], "batch", scatter_dimension=1, tiled=True),
        lax.psum_scatter(totals[4], "batch", scatter_dimension=1, tiled=True),
        lax.psum_scatter(totals[5], "batch", scatter_dimension=1, tiled=True),
        lax.psum_scatter(totals[6], "batch", scatter_dimension=0, tiled=True),
        lax.psum_scatter(totals[7], "batch", scatter_dimension=1, tiled=True),
    )
    summed = (
        lax.all_gather(shares[0].astype(jnp.bfloat16), "batch", axis=1, tiled=True).astype(
            jnp.float32
        ),
        lax.all_gather(shares[1].astype(jnp.bfloat16), "batch", axis=1, tiled=True).astype(
            jnp.float32
        ),
        lax.all_gather(shares[2].astype(jnp.bfloat16), "batch", axis=1, tiled=True).astype(
            jnp.float32
        ),
        lax.all_gather(shares[3].astype(jnp.bfloat16), "batch", axis=1, tiled=True).astype(
            jnp.float32
        ),
        lax.all_gather(shares[4].astype(jnp.bfloat16), "batch", axis=1, tiled=True).astype(
            jnp.float32
        ),
        lax.all_gather(shares[5].astype(jnp.bfloat16), "batch", axis=1, tiled=True).astype(
            jnp.float32
        ),
        lax.all_gather(shares[6].astype(jnp.bfloat16), "batch", axis=0, tiled=True).astype(
            jnp.float32
        ),
        lax.all_gather(shares[7].astype(jnp.bfloat16), "batch", axis=1, tiled=True).astype(
            jnp.float32
        ),
    )
    return (
        outputs[None],
        in_grads[None],
        summed[0][None],
        summed[1][None],
        summed[2][None],
        summed[3][None],
        summed[4][None],
        summed[5][None],
        summed[6][None],
        summed[7][None],
    )


def solution(mesh):
    return jax.shard_map(
        shards,
        mesh=mesh,
        in_specs=(
            P(None, "batch", None),
            P(None, "batch", None),
            P("batch"),
            P("batch"),
            P("pipe", None, None),
            P("pipe", None, None),
            P("pipe", None, None),
            P("pipe", None, None),
            P("pipe", None, None),
            P("pipe", None, None),
            P("pipe", None),
            P("pipe", None, None),
        ),
        out_specs=(
            P("pipe", None, "batch", None),
            P("pipe", None, "batch", None),
            P("pipe", None, None),
            P("pipe", None, None),
            P("pipe", None, None),
            P("pipe", None, None),
            P("pipe", None, None),
            P("pipe", None, None),
            P("pipe", None),
            P("pipe", None, None),
        ),
        check_vma=False,
    )
```

profile of v0, /device:TPU:0, one launch (start us, length us, event | category | flops | bytes accessed | tf_op | source)
XLA Modules:
  0.0 1343.5 jit_solution(17691376268064072097)
XLA Ops:
  48.1 7.8 fusion.276
  62.7 5.9 collective-permute-start
  95.1 6.1 broadcast_in_dim.512
  113.5 6.4 constant_dynamic-slice_fusion.12
  151.1 7.5 fusion.275
  184.6 9.7 bitcast_dynamic-update-slice_fusion.1
  198.5 6.4 constant_dynamic-slice_fusion.11
  236.1 6.7 fusion.293
  246.4 8.1 fusion.274
  264.1 6.4 multiply_reduce_fusion.5
  274.3 11.7 fusion.268
  313.6 5.7 dynamic-slice_bitcast_fusion
  331.1 7.2 multiply_reduce_fusion.2
  338.3 7.1 multiply_convert_fusion.2
  401.6 7.2 fusion.296
  409.4 6.4 fusion.297
  424.2 10.8 fusion.263
  435.1 7.1 multiply_reduce_fusion.18
  454.8 13.7 %multiply_reduce_fusion.1 = (f32[12,512]{1,0:T(8,128)S(1)}, f32[12,512,512]{1,2,0:T(8,128)}) fusion(f32[12,512,512]{1,2,0:T(8,128)} %fusion.296, f32[12,512]{1,0:T(8,128)} %get-tuple-element.373, pred[512,512]{0,1:T(8,128)(4,1)} %fusion.156, bf16[512,12,64]{0,2,1:T(8,128)(2,1)} %bitcast.779, bf16[512,12,64]{0,2,1:T(8,128)(2,1)} %bitcast.772), kind=kOutput, calls=%fused_computation.4 | convolution fusion | flops 418375680 | bytes 27049984 | tf_op jit(solution)/shard_map/while/body/eval_jaxpr/qhd,khd->hqk/dot_general | solution.py:101
  468.6 7.2 multiply_convert_fusion.1
  504.2 12.3 collective-permute-done.3
  523.7 6.4 convert_reduce_fusion
  530.2 7.0 multiply_reduce_fusion.15
  552.9 13.7 %multiply_reduce_fusion = (f32[12,512]{1,0:T(8,128)S(1)}, f32[12,512,512]{1,2,0:T(8,128)}) fusion(f32[12,512,512]{1,2,0:T(8,128)} %fusion.297, f32[12,512]{1,0:T(8,128)} %get-tuple-element.372, pred[512,512]{0,1:T(8,128)(4,1)} %fusion.155, bf16[512,12,64]{0,2,1:T(8,128)(2,1)} %bitcast.777, bf16[512,12,64]{0,2,1:T(8,128)(2,1)} %bitcast.771), kind=kOutput, calls=%fused_computation.1 | convolution fusion | flops 418375680 | bytes 27049984 | tf_op jit(solution)/shard_map/while/body/eval_jaxpr/qhd,khd->hqk/dot_general | solution.py:101
  566.7 7.5 multiply_convert_fusion
  581.0 8.4 select_add_fusion.2
  607.6 5.6 fusion.73
  613.2 8.6 select_add_fusion
  635.8 8.8 select_add_fusion.1
  687.8 22.6 %reduce-scatter.14.cloned.1.call-done = f32[768,144]{0,1:T(8,128)} async-done(((f32[768,2304]{0,1:T(8,128)}), f32[768,144]{0,1:T(8,128)}) %reduce-scatter.14.cloned.1.call-update) | async-done | bytes 442384 | tf_op jit(solution)/shard_map/reduce_scatter | solution.py:362
  712.2 113.8 %reduce-scatter.20.cloned.1.call-done = f32[3072,48]{0,1:T(8,128)} async-done(((f32[3072,768]{0,1:T(8,128)}), f32[3072,48]{0,1:T(8,128)}) %reduce-scatter.20.cloned.1.call-update) | async-done | bytes 589840 | tf_op jit(solution)/shard_map/reduce_scatter | solution.py:365
  827.9 114.3 %reduce-scatter.18.cloned.1.call-done = f32[768,192]{0,1:T(8,128)} async-done(((f32[768,3072]{0,1:T(8,128)}), f32[768,192]{0,1:T(8,128)}) %reduce-scatter.18.cloned.1.call-update) | async-done | bytes 589840 | tf_op jit(solution)/shard_map/reduce_scatter | solution.py:364
  948.4 7.1 fusion.137
  959.4 60.2 %all-reduce.1 = bf16[3072]{0:T(1024)(128)(2,1)} all-reduce(f32[3072]{0:T(1024)S(1)} %select_add_fusion.5), channel_id=8, replica_groups=mesh['pipe'=2,'batch'=16] {'batch'}, use_global_device_ids=true, to_apply=%region_118.119.clone | all-reduce | flops 3072 | bytes 18432
  1020.6 30.6 %all-reduce = bf16[3072]{0:T(1024)(128)(2,1)} all-reduce(bf16[3072]{0:T(1024)(128)(2,1)S(1)} %dynamic-update-slice), channel_id=1, replica_groups=mesh['pipe'=2,'batch'=16] {'batch'}, use_global_device_ids=true, to_apply=%add | all-reduce | flops 3072 | bytes 12288
  1058.9 17.1 %all-gather = bf16[16,48,3]{1,2,0:T(4,128)(2,1)S(1)} all-gather(bf16[1,48,3]{1,2,0:T(4,128)(2,1)S(1)} %bitcast.851), channel_id=1, replica_groups=mesh['pipe'=2,'batch'=16] {'batch'}, dimensions={0}, use_global_device_ids=true | all-gather | bytes 4896 | tf_op jit(solution)/shard_map/all_gather | solution.py:384
  1078.9 19.4 %all-gather.1 = bf16[16,48,7]{1,2,0:T(8,128)(2,1)S(1)} all-gather(bf16[1,48,7]{1,2,0:T(8,128)(2,1)S(1)} %bitcast.849), channel_id=1, replica_groups=mesh['pipe'=2,'batch'=16] {'batch'}, dimensions={0}, use_global_device_ids=true | all-gather | bytes 11424 | tf_op jit(solution)/shard_map/all_gather | solution.py:387
  1101.8 19.8 %reduce-scatter.26.cloned.1.call-done = f32[192,2]{1,0:T(8,128)} async-done(((f32[3072,2]{1,0:T(8,128)}), f32[192,2]{1,0:T(8,128)}) %reduce-scatter.26.cloned.1.call-update) | async-done | bytes 1552
  1122.6 19.6 %all-gather.2 = bf16[16,192,2]{1,2,0:T(2,128)(2,1)S(1)} all-gather(bf16[1,192,2]{1,2,0:T(2,128)(2,1)S(1)} %bitcast.850), channel_id=1, replica_groups=mesh['pipe'=2,'batch'=16] {'batch'}, dimensions={0}, use_global_device_ids=true | all-gather | bytes 13056 | tf_op jit(solution)/shard_map/all_gather | solution.py:393
  1144.2 17.9 %all-gather.10.cloned.1.call-done = bf16[768,768]{0,1:T(8,128)(2,1)} async-done(((bf16[768,48]{0,1:T(8,128)(2,1)}), bf16[768,768]{0,1:T(8,128)(2,1)}) %all-gather.10.cloned.1.call-update) | async-done | bytes 1179664 | tf_op jit(solution)/shard_map/all_gather | solution.py:375
  1168.0 42.8 %all-gather.8.cloned.1.call-done = bf16[768,2304]{0,1:T(8,128)(2,1)} async-done(((bf16[768,144]{0,1:T(8,128)(2,1)}), bf16[768,2304]{0,1:T(8,128)(2,1)}) %all-gather.8.cloned.1.call-update) | async-done | bytes 3538960 | tf_op jit(solution)/shard_map/all_gather | solution.py:372
  1216.3 8.0 copy.288
  1224.4 41.7 %all-gather.14.cloned.1.call-done = bf16[3072,768]{0,1:T(8,128)(2,1)} async-done(((bf16[3072,48]{0,1:T(8,128)(2,1)}), bf16[3072,768]{0,1:T(8,128)(2,1)}) %all-gather.14.cloned.1.call-update) | async-done | bytes 4718608 | tf_op jit(solution)/shard_map/all_gather | solution.py:381
  1266.1 7.4 bitcast_convert_fusion
  1273.4 9.7 copy.291
  1283.1 37.3 %all-gather.12.cloned.1.call-done = bf16[768,3072]{0,1:T(8,128)(2,1)} async-done(((bf16[768,192]{0,1:T(8,128)(2,1)}), bf16[768,3072]{0,1:T(8,128)(2,1)}) %all-gather.12.cloned.1.call-update) | async-done | bytes 4718608 | tf_op jit(solution)/shard_map/all_gather | solution.py:378
  1320.4 6.7 bitcast_convert_fusion.1
  1327.2 9.6 copy.290
  (1050 shorter events, 484.8 us)
Async XLA Ops:
  7.2 679.0 %reduce-scatter.16.cloned.1.call-start = ((), (), s32[]{:S(2)}) async-start(), calls=%async_computation.9 | async-start | bytes 2506752 | tf_op jit(solution)/shard_map/reduce_scatter | solution.py:363
  12.2 35.9 %copy-start.128 = (f32[768]{0:T(1024)}, f32[768]{0:T(1024)S(1)}, u32[]{:S(2)}) copy-start(f32[768]{0:T(1024)S(1)} %get-tuple-element.281) | copy-start | bytes 9220
  47.7 34.1 %copy-start.18 = (f32[512,768]{1,0:T(8,128)}, f32[512,768]{1,0:T(8,128)S(1)}, u32[]{:S(2)}) copy-start(f32[512,768]{1,0:T(8,128)S(1)} %get-tuple-element.396) | copy-start | bytes 4718596
  56.8 16.9 %slice-start.6 = ((s8[4718592]{0:T(1024)(128)(4,1)}), s8[4194304]{0:T(1024)(128)(4,1)S(1)}, s32[]{:S(2)}) async-start(s8[4718592]{0:T(1024)(128)(4,1)} %bitcast.725), calls=%async_computation.24 | async-start | bytes 8388608
  58.8 14.9 %slice-start.7 = ((s8[4718592]{0:T(1024)(128)(4,1)}), s8[524288]{0:T(1024)(128)(4,1)S(1)}, s32[]{:S(2)}) async-start(s8[4718592]{0:T(1024)(128)(4,1)} %bitcast.725), calls=%async_computation.25 | async-start | bytes 1048576
  62.7 15.2 %copy-start.54 = (bf16[2,512,768]{2,1,0:T(8,128)(2,1)}, bf16[2,512,768]{2,1,0:T(8,128)(2,1)S(1)}, u32[]{:S(2)}) copy-start(bf16[2,512,768]{2,1,0:T(8,128)(2,1)S(1)} %get-tuple-element.398) | copy-start | bytes 4718596
  62.7 57.2 %collective-permute-start = (bf16[512,768]{1,0:T(8,128)(2,1)}, bf16[512,768]{1,0:T(8,128)(2,1)}, u32[]{:S(2)}, u32[]{:S(2)}) collective-permute-start(bf16[512,768]{1,0:T(8,128)(2,1)} %get-tuple-element.399), channel_id=1, source_target_pairs={{0,16},{1,17},{2,18},{3,19},{4,20},{5,21},{6,22},{7,23},{8,24},{9,... | collective-permute-start | bytes 2359304 | tf_op jit(solution)/shard_map/ppermute | solution.py:16
  109.0 13.0 slice-start.8
  166.0 38.8 %collective-permute-start.1 = (bf16[512,768]{1,0:T(8,128)(2,1)}, bf16[512,768]{1,0:T(8,128)(2,1)}, u32[]{:S(2)}, u32[]{:S(2)}) collective-permute-start(bf16[512,768]{1,0:T(8,128)(2,1)} %get-tuple-element.408), channel_id=1, source_target_pairs={{0,16},{1,17},{2,18},{3,19},{4,20},{5,21},{6,22},{7,23},{8,24},{9,... | collective-permute-start | bytes 2359304 | tf_op jit(solution)/shard_map/ppermute | solution.py:16
  246.0 26.7 %copy-start.12 = (f32[512,768]{1,0:T(8,128)}, f32[512,768]{1,0:T(8,128)S(1)}, u32[]{:S(2)}) copy-start(f32[512,768]{1,0:T(8,128)S(1)} %get-tuple-element.414) | copy-start | bytes 4718596
  273.1 16.7 %copy-start.3 = (f32[2,512,768]{2,1,0:T(8,128)}, f32[2,512,768]{2,1,0:T(8,128)S(1)}, u32[]{:S(2)}) copy-start(f32[2,512,768]{2,1,0:T(8,128)S(1)} %bitcast_dynamic-update-slice_fusion.9) | copy-start | bytes 9437188
  273.1 12.9 slice-start.26
  348.6 15.6 %slice-start.14 = ((s8[6291456]{0:T(1024)(128)(4,1)}), s8[2097152]{0:T(1024)(128)(4,1)S(1)}, s32[]{:S(2)}) async-start(s8[6291456]{0:T(1024)(128)(4,1)} %bitcast.733), calls=%async_computation.32 | async-start | bytes 4194304
  351.9 12.3 slice-start.15
  362.7 53.2 %collective-permute-start.2 = (bf16[512,768]{1,0:T(8,128)(2,1)}, bf16[512,768]{1,0:T(8,128)(2,1)}, u32[]{:S(2)}, u32[]{:S(2)}) collective-permute-start(bf16[512,768]{1,0:T(8,128)(2,1)} %get-tuple-element.323), channel_id=1, source_target_pairs={{16,0},{17,1},{18,2},{19,3},{20,4},{21,5},{22,6},{23,7},{24,8},{25... | collective-permute-start | bytes 2359304 | tf_op jit(solution)/shard_map/ppermute | solution.py:16
  401.6 16.3 %slice-start.16 = ((s8[6291456]{0:T(1024)(128)(4,1)}), s8[4194304]{0:T(1024)(128)(4,1)S(1)}, s32[]{:S(2)}) async-start(s8[6291456]{0:T(1024)(128)(4,1)} %bitcast.735), calls=%async_computation.34 | async-start | bytes 8388608
  401.6 16.3 %slice-start.32 = ((s8[4718592]{0:T(1024)(128)(4,1)}), s8[4194304]{0:T(1024)(128)(4,1)S(1)}, s32[]{:S(2)}) async-start(s8[4718592]{0:T(1024)(128)(4,1)} %bitcast.858), calls=%async_computation.50 | async-start | bytes 8388608
  454.8 13.7 %slice-start.3 = ((s8[12582912]{0:T(1024)(128)(4,1)}), s8[4194304]{0:T(1024)(128)(4,1)S(1)}, s32[]{:S(2)}) async-start(s8[12582912]{0:T(1024)(128)(4,1)} %bitcast.723), calls=%async_computation.21 | async-start | bytes 8388608
  454.8 13.7 %slice-start.4 = ((s8[12582912]{0:T(1024)(128)(4,1)}), s8[4194304]{0:T(1024)(128)(4,1)S(1)}, s32[]{:S(2)}) async-start(s8[12582912]{0:T(1024)(128)(4,1)} %bitcast.723), calls=%async_computation.22 | async-start | bytes 8388608
  454.8 13.7 %slice-start.5 = ((s8[12582912]{0:T(1024)(128)(4,1)}), s8[4194304]{0:T(1024)(128)(4,1)S(1)}, s32[]{:S(2)}) async-start(s8[12582912]{0:T(1024)(128)(4,1)} %bitcast.723), calls=%async_computation.23 | async-start | bytes 8388608
  454.8 13.7 %copy-start.97 = (pred[512,512]{0,1:T(8,128)(4,1)S(1)}, pred[512,512]{0,1:T(8,128)(4,1)}, u32[]{:S(2)}) copy-start(pred[512,512]{0,1:T(8,128)(4,1)} %fusion.156) | copy-start | bytes 786436
  454.8 13.7 %copy-start.118 = (f32[12,512]{1,0:T(8,128)S(1)}, f32[12,512]{1,0:T(8,128)}, u32[]{:S(2)}) copy-start(f32[12,512]{1,0:T(8,128)} %get-tuple-element.373) | copy-start | bytes 73732
  476.9 18.7 %copy-start.66 = (bf16[12,64,512]{2,1,0:T(8,128)(2,1)}, bf16[12,64,512]{2,1,0:T(8,128)(2,1)S(1)}, u32[]{:S(2)}) copy-start(bf16[12,64,512]{2,1,0:T(8,128)(2,1)S(1)} %multiply_convert_fusion.6) | copy-start | bytes 2359300
  479.0 16.7 %copy-start.93 = (bf16[12,64,512]{2,1,0:T(8,128)(2,1)}, bf16[12,64,512]{2,1,0:T(8,128)(2,1)S(1)}, u32[]{:S(2)}) copy-start(bf16[12,64,512]{2,1,0:T(8,128)(2,1)S(1)} %multiply_convert_fusion.5) | copy-start | bytes 2359300
  481.7 14.0 %copy-start.108 = (bf16[12,64,512]{2,1,0:T(8,128)(2,1)}, bf16[12,64,512]{2,1,0:T(8,128)(2,1)S(1)}, u32[]{:S(2)}) copy-start(bf16[12,64,512]{2,1,0:T(8,128)(2,1)S(1)} %fusion.123) | copy-start | bytes 2359300
  492.8 24.7 %slice-start.18 = ((s8[6291456]{0:T(1024)(128)(4,1)}), s8[4194304]{0:T(1024)(128)(4,1)S(1)}, s32[]{:S(2)}) async-start(s8[6291456]{0:T(1024)(128)(4,1)} %bitcast.737), calls=%async_computation.36 | async-start | bytes 8388608
  492.9 24.7 %slice-start.34 = ((s8[4718592]{0:T(1024)(128)(4,1)}), s8[4194304]{0:T(1024)(128)(4,1)S(1)}, s32[]{:S(2)}) async-start(s8[4718592]{0:T(1024)(128)(4,1)} %bitcast.860), calls=%async_computation.52 | async-start | bytes 8388608
  494.1 22.5 %collective-permute-start.3 = (bf16[512,768]{1,0:T(8,128)(2,1)S(1)}, bf16[512,768]{1,0:T(8,128)(2,1)S(1)}, u32[]{:S(2)}, u32[]{:S(2)}) collective-permute-start(bf16[512,768]{1,0:T(8,128)(2,1)S(1)} %get-tuple-element.311), channel_id=1, source_target_pairs={{16,0},{17,1},{18,2},{19,3},{20,4},{21,5},{22,6},{23,7},{24,8},{25... | collective-permute-start | bytes 2359304 | tf_op jit(solution)/shard_map/ppermute | solution.py:16
  495.7 21.8 %slice-start.19 = ((s8[6291456]{0:T(1024)(128)(4,1)}), s8[2097152]{0:T(1024)(128)(4,1)S(1)}, s32[]{:S(2)}) async-start(s8[6291456]{0:T(1024)(128)(4,1)} %bitcast.737), calls=%async_computation.37 | async-start | bytes 4194304
  495.7 21.8 %slice-start.35 = ((s8[4718592]{0:T(1024)(128)(4,1)}), s8[524288]{0:T(1024)(128)(4,1)S(1)}, s32[]{:S(2)}) async-start(s8[4718592]{0:T(1024)(128)(4,1)} %bitcast.860), calls=%async_computation.53 | async-start | bytes 1048576
  500.7 15.8 %copy-start.32 = (bf16[2,512,768]{2,1,0:T(8,128)(2,1)S(1)}, bf16[2,512,768]{2,1,0:T(8,128)(2,1)}, u32[]{:S(2)}) copy-start(bf16[2,512,768]{2,1,0:T(8,128)(2,1)} %param.13) | copy-start | bytes 4718596
  500.8 15.8 %copy-start.172 = (f32[512]{0:T(512)S(1)}, f32[512]{0:T(512)}, u32[]{:S(2)}) copy-start(f32[512]{0:T(512)} %fusion.249) | copy-start | bytes 6148
  552.8 157.6 %reduce-scatter.14.cloned.1.call-start = ((), (), s32[]{:S(2)}) async-start(), calls=%async_computation.7 | async-start | bytes 7520256 | tf_op jit(solution)/shard_map/reduce_scatter | solution.py:362
  552.9 13.7 %slice-start = ((s8[12582912]{0:T(1024)(128)(4,1)}), s8[4194304]{0:T(1024)(128)(4,1)S(1)}, s32[]{:S(2)}) async-start(s8[12582912]{0:T(1024)(128)(4,1)} %bitcast.721), calls=%async_computation.18 | async-start | bytes 8388608
  552.9 13.7 %slice-start.1 = ((s8[12582912]{0:T(1024)(128)(4,1)}), s8[4194304]{0:T(1024)(128)(4,1)S(1)}, s32[]{:S(2)}) async-start(s8[12582912]{0:T(1024)(128)(4,1)} %bitcast.721), calls=%async_computation.19 | async-start | bytes 8388608
  552.9 13.7 %slice-start.2 = ((s8[12582912]{0:T(1024)(128)(4,1)}), s8[4194304]{0:T(1024)(128)(4,1)S(1)}, s32[]{:S(2)}) async-start(s8[12582912]{0:T(1024)(128)(4,1)} %bitcast.721), calls=%async_computation.20 | async-start | bytes 8388608
  552.9 13.7 %copy-start.96 = (pred[512,512]{0,1:T(8,128)(4,1)S(1)}, pred[512,512]{0,1:T(8,128)(4,1)}, u32[]{:S(2)}) copy-start(pred[512,512]{0,1:T(8,128)(4,1)} %fusion.155) | copy-start | bytes 786436
  552.9 13.7 %copy-start.117 = (f32[12,512]{1,0:T(8,128)S(1)}, f32[12,512]{1,0:T(8,128)}, u32[]{:S(2)}) copy-start(f32[12,512]{1,0:T(8,128)} %get-tuple-element.372) | copy-start | bytes 73732
  589.4 236.6 %reduce-scatter.20.cloned.1.call-start = ((), (), s32[]{:S(2)}) async-start(), calls=%async_computation.13 | async-start | bytes 10027008 | tf_op jit(solution)/shard_map/reduce_scatter | solution.py:365
  621.8 320.4 %reduce-scatter.18.cloned.1.call-start = ((), (), s32[]{:S(2)}) async-start(), calls=%async_computation.11 | async-start | bytes 10027008 | tf_op jit(solution)/shard_map/reduce_scatter | solution.py:364
  644.6 413.6 %reduce-scatter.22.cloned.1.call-start = ((), (), s32[]{:S(2)}) async-start(), calls=%async_computation.15 | async-start | bytes 417792
  653.6 13.3 copy-start.127
  677.7 400.4 %reduce-scatter.24.cloned.1.call-start = ((), (), s32[]{:S(2)}) async-start(), calls=%async_computation.16 | async-start | bytes 417792
  682.2 439.4 %reduce-scatter.26.cloned.1.call-start = ((), (), s32[]{:S(2)}) async-start(), calls=%async_computation.17 | async-start | bytes 1671168
  686.1 476.0 %all-gather.10.cloned.1.call-start = ((), (), s32[]{:S(2)}) async-start(), calls=%async_computation.10 | async-start | bytes 1253376 | tf_op jit(solution)/shard_map/all_gather | solution.py:375
  687.8 523.1 %all-gather.8.cloned.1.call-start = ((), (), s32[]{:S(2)}) async-start(), calls=%async_computation.8 | async-start | bytes 3760128 | tf_op jit(solution)/shard_map/all_gather | solution.py:372
  712.2 553.9 %all-gather.14.cloned.1.call-start = ((), (), s32[]{:S(2)}) async-start(), calls=%async_computation.14 | async-start | bytes 5013504 | tf_op jit(solution)/shard_map/all_gather | solution.py:381
  827.8 492.6 %all-gather.12.cloned.1.call-start = ((), (), s32[]{:S(2)}) async-start(), calls=%async_computation.12 | async-start | bytes 5013504 | tf_op jit(solution)/shard_map/all_gather | solution.py:378
  (299 other events, 1302.5 us)
Sparse Core Ops, SparseCore 0:
  552.9 63.2 reduce-scatter.15
  621.4 89.0 reduce-scatter.13
  715.1 110.8 reduce-scatter.19
  831.1 111.0 reduce-scatter.17
  945.5 55.3 reduce-scatter.21
  1004.7 54.5 reduce-scatter.23
  1063.0 58.5 reduce-scatter.25
  1124.7 37.3 all-gather.9
  1164.7 46.1 all-gather.7
  1213.8 52.2 all-gather.13
  1268.6 51.7 all-gather.11
where the time goes:
time: 1360 us; the launch traced here: 1340 us
  waiting for transfers between devices  423 us (31%)
  matrix products  269 us (20%)
  other arithmetic  251 us (18%)
  local copies, waits for them, and re-layouts  221 us (16%)
  blocking collectives  147 us (11%)
  between operations  19.6 us (1%)
    reduce_scatter x1, waiting for transfers between devices, shards(): lax.psum_scatter(totals[2], 'batch', scatter_dimension=1, tiled=True)  114 us
    reduce_scatter x1, waiting for transfers between devices, shards(): lax.psum_scatter(totals[3], 'batch', scatter_dimension=1, tiled=True)  114 us
    unnamed x2, blocking collectives  90.8 us
    unnamed x682, local copies, waits for them, and re-layouts  74.6 us
    dot_general x12, matrix products, multiply_left_t(): lax.dot_general(left, right, (((0,), (0,)), ((), ())), preferred_element_...  64.3 us
    dynamic_update_slice x29, other arithmetic, put_slot(): lax.dynamic_update_index_in_dim(buffer, jnp.where(usable, new_value, prev...  63.3 us
    dot_general x12, matrix products, multiply_right_t(): lax.dot_general(left, right, (((1,), (1,)), ((), ())), preferred_element_...  59.8 us
    reduce_sum x20, other arithmetic, normalize(): centred = values_in - jnp.mean(values_in, axis=-1, keepdims=True)  59.8 us
  transfers between devices with their start and end apart: 15, of which 9 were waited for; matrix products, arithmetic and copies ran while one was open for 25% of the time, Pallas kernels for 0%

commit v1 on v0

v1 whole, which is shorter than its diff:
```python
import functools

import jax
import jax.numpy as jnp
from jax import lax
from jax.experimental import pallas as pl
from jax.experimental.pallas import tpu as pltpu
from jax.sharding import PartitionSpec as P

HEAD = 64
PAIR = 2 * HEAD
EPSILON = 1e-05
SCALE = 0.125
HIDDEN_NEG = -1e30
CHUNK = 512
SUM_ROWS = 32
TILE = 16
VMEM_BYTES = 56 * 1024 * 1024
MESH_IDS = pl.DeviceIdType.MESH


def dot_nn(left, right):
    return jnp.dot(left, right, preferred_element_type=jnp.float32)


def dot_nt(left, right):
    return lax.dot_general(
        left, right, (((1,), (1,)), ((), ())), preferred_element_type=jnp.float32
    )


def dot_tn(left, right):
    return lax.dot_general(
        left, right, (((0,), (0,)), ((), ())), preferred_element_type=jnp.float32
    )


def standardize(values_in):
    centred = values_in - jnp.mean(values_in, axis=-1, keepdims=True)
    scale = lax.rsqrt(jnp.mean(centred * centred, axis=-1, keepdims=True) + EPSILON)
    return centred * scale, scale


def row_blocks(total, size, body):
    def one(index, carry):
        body(pl.ds(pl.multiple_of(index * size, size), size))
        return carry

    lax.fori_loop(0, total // size, one, 0)


FWD_STATE = ("normed_in", "projected", "log_total", "attended", "normed_mix", "residual",
             "normed_ffn", "normed_hidden", "slope", "spread")


def state_shapes(rows, width, hidden):
    bf, f = jnp.bfloat16, jnp.float32
    return {
        "normed_in": ((rows, width), bf),
        "projected": ((rows, 3 * width), bf),
        "log_total": ((PAIR, rows), f),
        "attended": ((rows, width), f),
        "normed_mix": ((rows, width), bf),
        "residual": ((rows, width), f),
        "normed_ffn": ((rows, width), bf),
        "normed_hidden": ((rows, hidden), bf),
        "slope": ((rows, hidden), bf),
        "spread": ((rows, PAIR), f),
    }


def forward_kernel(
    aliased, flag_ref, length_ref, x_hbm, wq_hbm, wo_hbm, wu_hbm, wd_hbm, gm, sm, gh, sh, *refs
):
    count = 1 + len(FWD_STATE)
    if aliased:
        refs = refs[count:]
    outs, scratch = refs[:count], refs[count:]
    y_hbm, state_hbm = outs[0], dict(zip(FWD_STATE, outs[1:]))
    (x_s, wq, wo, wu, wd, y_s) = scratch[:6]
    held = dict(zip(FWD_STATE, scratch[6 : 6 + len(FWD_STATE)]))
    (act_s, bias_s, in_sem, out_sem) = scratch[6 + len(FWD_STATE) :]
    rows, width = x_s.shape
    hidden = wu.shape[1]
    heads = width // HEAD

    @pl.when(flag_ref[0] == 1)
    def _():
        loads = [
            pltpu.make_async_copy(source, target, in_sem.at[at])
            for at, (source, target) in enumerate(
                [(x_hbm, x_s), (wq_hbm, wq), (wo_hbm, wo), (wu_hbm, wu), (wd_hbm, wd)]
            )
        ]
        for item in loads:
            item.start()
        stores = {
            name: pltpu.make_async_copy(held[name], state_hbm[name], out_sem.at[at])
            for at, name in enumerate(FWD_STATE)
        }
        store_y = pltpu.make_async_copy(y_s, y_hbm, out_sem.at[len(FWD_STATE)])

        length = length_ref[0]
        query = lax.broadcasted_iota(jnp.int32, (rows, rows), 0)
        key = lax.broadcasted_iota(jnp.int32, (rows, rows), 1)
        visible = (key <= query) & ((key < length) | (key == query))
        bias_s[...] = jnp.where(visible, 0.0, HIDDEN_NEG)

        loads[0].wait()
        loads[1].wait()

        def project(at):
            unit, unused = standardize(x_s[at, :].astype(jnp.float32))
            normed = (unit * gm[0:1, :] + sm[0:1, :]).astype(jnp.bfloat16)
            held["normed_in"][at, :] = normed
            for block in range(3):
                cols = pl.ds(block * width, width)
                out = dot_nn(normed, wq[:, cols])
                if block != 1:
                    out = out + sm[1 + block // 2 : 2 + block // 2, :]
                held["projected"][at, cols] = out.astype(jnp.bfloat16)

        project(slice(None))
        stores["normed_in"].start()
        stores["projected"].start()

        half = rows // 2
        lane = lax.broadcasted_iota(jnp.int32, (half, PAIR), 1)

        def attend(pair, totals):
            first = pl.multiple_of(pair * PAIR, PAIR)
            new_totals = []
            for block in range(2):
                at = pl.ds(block * half, half)
                reach = (block + 1) * half
                q = held["projected"][at, pl.ds(first, PAIR)] * jnp.bfloat16(SCALE)
                k = held["projected"][0:reach, pl.ds(width + first, PAIR)]
                v = held["projected"][0:reach, pl.ds(2 * width + first, PAIR)]
                mixed = []
                total = totals[block]
                for which in range(2):
                    mine = (lane >= HEAD) if which else (lane < HEAD)
                    scores = dot_nt(jnp.where(mine, q, jnp.zeros_like(q)), k)
                    scores = scores + bias_s[at, 0:reach]
                    top = jnp.max(scores, axis=-1, keepdims=True)
                    exps = jnp.exp(scores - top)
                    row_sum = jnp.sum(exps, axis=-1, keepdims=True)
                    out = dot_nn(exps.astype(jnp.bfloat16), v)
                    mixed.append(out * (1.0 / row_sum))
                    total = jnp.where(lane == 2 * pair + which, top + jnp.log(row_sum), total)
                held["attended"][at, pl.ds(first, PAIR)] = jnp.where(
                    lane < HEAD, mixed[0], mixed[1]
                )
                new_totals.append(total)
            return tuple(new_totals)

        zero = jnp.zeros((half, PAIR), jnp.float32)
        totals = lax.fori_loop(0, heads // 2, attend, (zero, zero))
        for block in range(2):
            held["log_total"][:, block * half : (block + 1) * half] = totals[block].T
        stores["log_total"].start()
        stores["attended"].start()

        loads[2].wait()

        unit, unused = standardize(held["attended"][...])
        normed_mix = (unit * gm[1:2, :] + sm[3:4, :]).astype(jnp.bfloat16)
        held["normed_mix"][...] = normed_mix
        stores["normed_mix"].start()
        residual = x_s[...].astype(jnp.float32) + dot_nn(normed_mix, wo[...]) + sm[4:5, :]
        held["residual"][...] = residual
        stores["residual"].start()
        unit, unused = standardize(residual)
        normed_ffn = (unit * gm[2:3, :] + sm[5:6, :]).astype(jnp.bfloat16)
        held["normed_ffn"][...] = normed_ffn
        stores["normed_ffn"].start()
        loads[3].wait()
        total = jnp.zeros((rows, 1), jnp.float32)
        for first in range(0, hidden, CHUNK):
            cols = slice(first, first + CHUNK)
            pre = dot_nn(held["normed_ffn"][...], wu[:, cols]) + sh[0:1, cols]
            share = 0.5 + 0.5 * lax.erf(pre * 0.7071067811865476)
            density = 0.3989422804014327 * jnp.exp(-0.5 * pre * pre)
            act = pre * share
            held["slope"][:, cols] = (share + pre * density).astype(jnp.bfloat16)
            act_s[:, cols] = act
            total = total + jnp.sum(act, axis=-1, keepdims=True)
        stores["slope"].start()
        mean = total * (1.0 / hidden)
        square = jnp.zeros((rows, 1), jnp.float32)
        for first in range(0, hidden, CHUNK):
            centred = act_s[:, first : first + CHUNK] - mean
            square = square + jnp.sum(centred * centred, axis=-1, keepdims=True)
        scale = lax.rsqrt(square * (1.0 / hidden) + EPSILON)
        held["spread"][...] = jnp.broadcast_to(scale, (rows, PAIR))
        stores["spread"].start()
        for first in range(0, hidden, CHUNK):
            cols = slice(first, first + CHUNK)
            unit = (act_s[:, cols] - mean) * scale
            held["normed_hidden"][:, cols] = (
                unit * gh[0:1, cols] + sh[1:2, cols]
            ).astype(jnp.bfloat16)
        stores["normed_hidden"].start()
        loads[4].wait()
        out = held["residual"][...] + dot_nn(held["normed_hidden"][...], wd[...]) + sm[6:7, :]
        y_s[...] = out.astype(jnp.bfloat16)
        store_y.start()
        for name in FWD_STATE:
            stores[name].wait()
        store_y.wait()


def forward_call(flag, length, x, weights, previous=None):
    wq, wo, wu, wd, gm, sm, gh, sh = weights
    rows, width = x.shape
    hidden = wu.shape[1]
    shapes = state_shapes(rows, width, hidden)
    out_shape = [jax.ShapeDtypeStruct((rows, width), jnp.bfloat16)]
    out_shape += [jax.ShapeDtypeStruct(*shapes[name]) for name in FWD_STATE]
    any_spec = pl.BlockSpec(memory_space=pl.ANY)
    vmem_spec = pl.BlockSpec(memory_space=pltpu.VMEM)
    smem_spec = pl.BlockSpec(memory_space=pltpu.SMEM)
    in_specs = [smem_spec] * 2 + [any_spec] * 5 + [vmem_spec] * 4
    args = [flag, length, x, wq, wo, wu, wd, gm, sm, gh, sh]
    aliases = {}
    if previous is not None:
        aliases = {len(args) + at: at for at in range(len(previous))}
        in_specs += [any_spec] * len(previous)
        args += list(previous)
    bf = jnp.bfloat16
    scratch = [pltpu.VMEM(item.shape, bf) for item in (x, wq, wo, wu, wd, x)]
    scratch += [pltpu.VMEM(*shapes[name]) for name in FWD_STATE]
    scratch += [
        pltpu.VMEM((rows, hidden), jnp.float32),
        pltpu.VMEM((rows, rows), jnp.float32),
        pltpu.SemaphoreType.DMA((5,)),
        pltpu.SemaphoreType.DMA((len(FWD_STATE) + 1,)),
    ]
    return pl.pallas_call(
        functools.partial(forward_kernel, previous is not None),
        out_shape=out_shape,
        in_specs=in_specs,
        out_specs=[any_spec] * len(out_shape),
        input_output_aliases=aliases,
        scratch_shapes=scratch,
        compiler_params=pltpu.CompilerParams(vmem_limit_bytes=VMEM_BYTES),
        cost_estimate=pl.CostEstimate(
            flops=2 * rows * width * (3 * width + width + 2 * hidden),
            bytes_accessed=40_000_000,
            transcendentals=0,
        ),
    )(*args)


BWD_STATE = ("d_down", "d_pre", "d_branch", "d_proj", "sums")


def backward_shapes(rows, width, hidden):
    bf = jnp.bfloat16
    return {
        "d_down": ((rows, width), bf),
        "d_pre": ((rows, hidden), bf),
        "d_branch": ((rows, width), bf),
        "d_proj": ((rows, 3 * width), bf),
        "sums": ((SUM_ROWS, width), jnp.float32),
    }


def unit_backward(grad, unit, scale, gain):
    scaled = grad * gain
    first = jnp.mean(scaled, axis=-1, keepdims=True)
    second = jnp.mean(scaled * unit, axis=-1, keepdims=True)
    return (
        scale * (scaled - first - unit * second),
        jnp.sum(grad * unit, axis=0, keepdims=True),
        jnp.sum(grad, axis=0, keepdims=True),
    )


def column_sum(values):
    return jnp.sum(values.astype(jnp.float32), axis=0, keepdims=True)


def backward_kernel(
    aliased, masked, flag_ref, length_ref, dy_hbm, x_hbm, wq_hbm, wo_hbm, wu_hbm, wd_hbm, gm, sm,
    gh, sh, projected_hbm, log_total_hbm, attended_hbm, residual_hbm, normed_hidden_hbm, slope_hbm,
    spread_hbm, *refs
):
    count = 1 + len(BWD_STATE)
    if aliased:
        refs = refs[count:]
    outs, scratch = refs[:count], refs[count:]
    dx_hbm, out_hbm = outs[0], dict(zip(BWD_STATE, outs[1:]))
    (dy_s, x_s, wq, wo, wu, wd, projected, log_total, attended, residual, normed_hidden, slope,
     spread, dx_s) = scratch[:14]
    held = dict(zip(BWD_STATE, scratch[14 : 14 + len(BWD_STATE)]))
    (e_s, d_residual, d_attended, delta_s, bias_s, in_sem, out_sem) = scratch[14 + len(BWD_STATE) :]
    rows, width = dx_s.shape
    hidden = wu.shape[1]
    heads = width // HEAD
    wide = hidden // width

    @pl.when(flag_ref[0] == 1)
    def _():
        order = [
            (dy_hbm, dy_s), (wd_hbm, wd), (normed_hidden_hbm, normed_hidden),
            (slope_hbm, slope), (spread_hbm, spread), (wu_hbm, wu), (residual_hbm, residual),
            (wo_hbm, wo), (attended_hbm, attended), (projected_hbm, projected),
            (log_total_hbm, log_total), (wq_hbm, wq), (x_hbm, x_s),
        ]
        loads = [
            pltpu.make_async_copy(source, target, in_sem.at[at])
            for at, (source, target) in enumerate(order)
        ]
        for item in loads:
            item.start()
        stores = {
            name: pltpu.make_async_copy(held[name], out_hbm[name], out_sem.at[at])
            for at, name in enumerate(BWD_STATE)
        }
        store_dx = pltpu.make_async_copy(dx_s, dx_hbm, out_sem.at[len(BWD_STATE)])
        sums = held["sums"]
        sums[...] = jnp.zeros_like(sums)

        length = length_ref[0]
        query = lax.broadcasted_iota(jnp.int32, (rows, rows), 1)
        key = lax.broadcasted_iota(jnp.int32, (rows, rows), 0)
        visible = (key <= query) & ((key < length) | (key == query))
        bias_s[...] = jnp.where(visible, 0.0, HIDDEN_NEG)

        loads[0].wait()
        if masked:
            live = lax.broadcasted_iota(jnp.int32, (rows, 1), 0) < length
            dy_s[...] = jnp.where(live, dy_s[...].astype(jnp.float32), 0.0).astype(jnp.bfloat16)
        held["d_down"][...] = dy_s[...]
        stores["d_down"].start()
        sums[9:10, :] = column_sum(dy_s[...])
        for item in loads[1:5]:
            item.wait()

        scale = spread[:, 0:1]
        first_total = jnp.zeros((rows, 1), jnp.float32)
        second_total = jnp.zeros((rows, 1), jnp.float32)
        for block in range(wide):
            cols = slice(block * width, (block + 1) * width)
            grad = dot_nt(dy_s[...], wd[cols, :])
            unit = (normed_hidden[:, cols].astype(jnp.float32) - sh[1:2, cols]) * gh[1:2, cols]
            sums[10 + block : 11 + block, :] = jnp.sum(grad * unit, axis=0, keepdims=True)
            sums[18 + block : 19 + block, :] = jnp.sum(grad, axis=0, keepdims=True)
            scaled = grad * gh[0:1, cols]
            e_s[:, cols] = scaled
            first_total = first_total + jnp.sum(scaled, axis=-1, keepdims=True)
            second_total = second_total + jnp.sum(scaled * unit, axis=-1, keepdims=True)
        first_mean = first_total * (1.0 / hidden)
        second_mean = second_total * (1.0 / hidden)
        for block in range(wide):
            cols = slice(block * width, (block + 1) * width)
            unit = (normed_hidden[:, cols].astype(jnp.float32) - sh[1:2, cols]) * gh[1:2, cols]
            d_act = scale * (e_s[:, cols] - first_mean - unit * second_mean)
            d_pre = (d_act * slope[:, cols].astype(jnp.float32)).astype(jnp.bfloat16)
            held["d_pre"][:, cols] = d_pre
            sums[14 + block : 15 + block, :] = column_sum(d_pre)
        stores["d_pre"].start()

        loads[5].wait()
        loads[6].wait()
        d_ffn = dot_nt(held["d_pre"][...], wu[...])
        unit, scale = standardize(residual[...])
        through, gain_sum, shift_sum = unit_backward(d_ffn, unit, scale, gm[2:3, :])
        sums[2:3, :] = gain_sum
        sums[8:9, :] = shift_sum
        through = through + dy_s[...].astype(jnp.float32)
        d_residual[...] = through
        held["d_branch"][...] = through.astype(jnp.bfloat16)
        stores["d_branch"].start()
        sums[7:8, :] = column_sum(held["d_branch"][...])

        loads[7].wait()
        loads[8].wait()
        d_mix = dot_nt(held["d_branch"][...], wo[...])
        unit, scale = standardize(attended[...])
        through, gain_sum, shift_sum = unit_backward(d_mix, unit, scale, gm[1:2, :])
        sums[1:2, :] = gain_sum
        sums[6:7, :] = shift_sum
        d_attended[...] = through.astype(jnp.bfloat16)
        product = d_attended[...].astype(jnp.float32) * attended[...]
        upper = product.astype(jnp.bfloat16)
        lower = (product - upper.astype(jnp.float32)).astype(jnp.bfloat16)
        head_row = lax.broadcasted_iota(jnp.int32, (16, width), 0)
        head_col = lax.broadcasted_iota(jnp.int32, (16, width), 1) // HEAD
        chooser = jnp.where(head_row == head_col, 1.0, 0.0).astype(jnp.bfloat16)
        delta_s[...] = dot_nt(chooser, upper) + dot_nt(chooser, lower)

        loads[9].wait()
        loads[10].wait()
        half = rows // 2
        lane = lax.broadcasted_iota(jnp.int32, (half, PAIR), 1)
        spot = lax.broadcasted_iota(jnp.int32, (PAIR, rows), 0)

        def attend(pair, carry):
            first = pl.multiple_of(pair * PAIR, PAIR)
            k_all = projected[:, pl.ds(width + first, PAIR)]
            v_all = projected[:, pl.ds(2 * width + first, PAIR)]
            k_turned = k_all.T
            dk = [None, None]
            dv = [None, None]
            for block in range(2):
                at = slice(block * half, (block + 1) * half)
                reach = (block + 1) * half
                q = projected[at, pl.ds(first, PAIR)] * jnp.bfloat16(SCALE)
                grad = d_attended[at, pl.ds(first, PAIR)]
                dq_turned = None
                for which in range(2):
                    mine = (lane >= HEAD) if which else (lane < HEAD)
                    own = (spot >= HEAD) if which else (spot < HEAD)
                    q_own = jnp.where(mine, q, jnp.zeros_like(q))
                    grad_own = jnp.where(mine, grad, jnp.zeros_like(grad))
                    scores = dot_nt(k_all[0:reach], q_own) + bias_s[0:reach, at]
                    head = pl.ds(2 * pair + which, 1)
                    probs = jnp.exp(scores - log_total[head, at])
                    d_probs = dot_nt(v_all[0:reach], grad_own)
                    d_scores = (probs * (d_probs - delta_s[head, at])).astype(jnp.bfloat16)
                    more_v = dot_nn(probs.astype(jnp.bfloat16), grad_own)
                    more_k = dot_nn(d_scores, q_own)
                    for part in range(block + 1):
                        piece = slice(part * half, (part + 1) * half)
                        dv[part] = more_v[piece] if dv[part] is None else dv[part] + more_v[piece]
                        dk[part] = more_k[piece] if dk[part] is None else dk[part] + more_k[piece]
                    k_own = jnp.where(own, k_turned, jnp.zeros_like(k_turned))[:, 0:reach]
                    more_q = dot_nn(k_own, d_scores)
                    dq_turned = more_q if dq_turned is None else dq_turned + more_q
                held["d_proj"][at, pl.ds(first, PAIR)] = (dq_turned.T * SCALE).astype(jnp.bfloat16)
            for part in range(2):
                at = slice(part * half, (part + 1) * half)
                held["d_proj"][at, pl.ds(width + first, PAIR)] = dk[part].astype(jnp.bfloat16)
                held["d_proj"][at, pl.ds(2 * width + first, PAIR)] = dv[part].astype(jnp.bfloat16)
            return carry

        lax.fori_loop(0, heads // 2, attend, 0)
        stores["d_proj"].start()

        loads[11].wait()
        loads[12].wait()
        d_norm = dot_nt(held["d_proj"][...], wq[...])
        sums[4:5, :] = column_sum(held["d_proj"][:, 0:width])
        sums[5:6, :] = column_sum(held["d_proj"][:, 2 * width :])
        unit, scale = standardize(x_s[...].astype(jnp.float32))
        through, gain_sum, shift_sum = unit_backward(d_norm, unit, scale, gm[0:1, :])
        sums[0:1, :] = gain_sum
        sums[3:4, :] = shift_sum
        dx_s[...] = (through + d_residual[...]).astype(jnp.bfloat16)
        store_dx.start()
        stores["sums"].start()
        for name in BWD_STATE:
            stores[name].wait()
        store_dx.wait()


def backward_call(flag, length, dy, x, weights, state, masked, previous=None):
    wq, wo, wu, wd, gm, sm, gh, sh = weights
    rows, width = x.shape
    hidden = wu.shape[1]
    shapes = backward_shapes(rows, width, hidden)
    bf = jnp.bfloat16
    out_shape = [jax.ShapeDtypeStruct((rows, width), bf)]
    out_shape += [jax.ShapeDtypeStruct(*shapes[name]) for name in BWD_STATE]
    any_spec = pl.BlockSpec(memory_space=pl.ANY)
    vmem_spec = pl.BlockSpec(memory_space=pltpu.VMEM)
    smem_spec = pl.BlockSpec(memory_space=pltpu.SMEM)
    kept = [state[name] for name in ("projected", "log_total", "attended", "residual",
                                     "normed_hidden", "slope", "spread")]
    in_specs = [smem_spec] * 2 + [any_spec] * 6 + [vmem_spec] * 4 + [any_spec] * len(kept)
    args = [flag, length, dy, x, wq, wo, wu, wd, gm, sm, gh, sh] + kept
    aliases = {}
    if previous is not None:
        aliases = {len(args) + at: at for at in range(len(previous))}
        in_specs += [any_spec] * len(previous)
        args += list(previous)
    scratch = [pltpu.VMEM(item.shape, item.dtype) for item in [dy, x, wq, wo, wu, wd] + kept + [x]]
    scratch += [pltpu.VMEM(*shapes[name]) for name in BWD_STATE]
    scratch += [
        pltpu.VMEM((rows, hidden), jnp.float32),
        pltpu.VMEM((rows, width), jnp.float32),
        pltpu.VMEM((rows, width), bf),
        pltpu.VMEM((16, rows), jnp.float32),
        pltpu.VMEM((rows, rows), jnp.float32),
        pltpu.SemaphoreType.DMA((13,)),
        pltpu.SemaphoreType.DMA((len(BWD_STATE) + 1,)),
    ]
    return pl.pallas_call(
        functools.partial(backward_kernel, previous is not None, masked),
        out_shape=out_shape,
        in_specs=in_specs,
        out_specs=[any_spec] * len(out_shape),
        input_output_aliases=aliases,
        scratch_shapes=scratch,
        compiler_params=pltpu.CompilerParams(vmem_limit_bytes=VMEM_BYTES),
        cost_estimate=pl.CostEstimate(
            flops=2 * rows * width * (3 * width + width + 2 * hidden),
            bytes_accessed=40_000_000,
            transcendentals=0,
        ),
    )(*args)


LEFT = ("normed_hidden", "normed_ffn", "normed_mix", "normed_in")
RIGHT = ("d_down", "d_pre", "d_branch", "d_proj")


def weight_grad_kernel(micro_count, *refs):
    parts = len(LEFT)
    sources = [refs[slot * 9 : slot * 9 + 9] for slot in range(micro_count)]
    out_hbm = refs[micro_count * 9]
    scratch = refs[micro_count * 9 + 1 :]
    left, right = scratch[0:parts], scratch[parts : 2 * parts]
    sums, out_s, turned, in_sem, out_sem = scratch[2 * parts :]
    tokens, width = left[3].shape
    rows = tokens // micro_count
    hidden = left[0].shape[1]
    wide = hidden // width
    loads = []
    for part in range(parts):
        for slot in range(micro_count):
            at = pl.ds(slot * rows, rows)
            for side, target in ((0, left[part]), (parts, right[part])):
                loads.append(
                    pltpu.make_async_copy(
                        sources[slot][side + part], target.at[at], in_sem.at[len(loads)]
                    )
                )
    for slot in range(micro_count):
        loads.append(
            pltpu.make_async_copy(sources[slot][2 * parts], sums.at[slot], in_sem.at[len(loads)])
        )
    for item in loads:
        item.start()
    starts = {"normed_in": 0, "normed_mix": 3, "normed_ffn": 4, "normed_hidden": 4 + wide}
    stores = []

    def store(first, count):
        at = pl.ds(first, count)
        stores.append(pltpu.make_async_copy(out_s.at[at], out_hbm.at[at], out_sem.at[len(stores)]))
        stores[-1].start()

    for part, name in enumerate(LEFT):
        for item in loads[2 * micro_count * part : 2 * micro_count * (part + 1)]:
            item.wait()
        first = starts[name] * width
        if name == "normed_hidden":

            def one(block, carry):
                cols = pl.ds(pl.multiple_of(block * width, width), width)
                turned[...] = left[part][:, cols].T
                at = pl.ds(pl.multiple_of(first + block * width, width), width)
                out_s[at, :] = dot_nn(turned[...], right[part][...]).astype(jnp.bfloat16)
                return carry

            lax.fori_loop(0, wide, one, 0)
            store(first, wide * width)
        else:
            turned[...] = left[part][...].T
            blocks = right[part].shape[1] // width

            def one(block, carry):
                cols = pl.ds(pl.multiple_of(block * width, width), width)
                at = pl.ds(pl.multiple_of(first + block * width, width), width)
                out_s[at, :] = dot_nn(turned[...], right[part][:, cols]).astype(jnp.bfloat16)
                return carry

            lax.fori_loop(0, blocks, one, 0)
            store(first, blocks * width)
    for item in loads[2 * micro_count * parts :]:
        item.wait()
    total = sums[0]
    for slot in range(1, micro_count):
        total = total + sums[slot]
    first = (4 + 2 * wide) * width
    out_s[first : first + SUM_ROWS, :] = total.astype(jnp.bfloat16)
    rest = out_s.shape[0] - first - SUM_ROWS
    if rest:
        out_s[first + SUM_ROWS :, :] = jnp.zeros((rest, width), jnp.bfloat16)
    store(first, SUM_ROWS + rest)
    for item in stores:
        item.wait()


def weight_grads(forward_states, backward_states, devices):
    micro_count = len(forward_states)
    args = []
    for kept, grads in zip(forward_states, backward_states):
        args += [kept[name] for name in LEFT] + [grads[name] for name in RIGHT] + [grads["sums"]]
    rows, width = forward_states[0]["normed_in"].shape
    hidden = forward_states[0]["normed_hidden"].shape[1]
    used = (4 + 2 * hidden // width) * width + SUM_ROWS
    unit = TILE * devices
    total_rows = used + -used % unit
    bf = jnp.bfloat16
    any_spec = pl.BlockSpec(memory_space=pl.ANY)
    scratch = [pltpu.VMEM((micro_count * rows, item.shape[1]), bf) for item in args[:8]]
    scratch += [
        pltpu.VMEM((micro_count, SUM_ROWS, width), jnp.float32),
        pltpu.VMEM((total_rows, width), bf),
        pltpu.VMEM((width, micro_count * rows), bf),
        pltpu.SemaphoreType.DMA((len(args),)),
        pltpu.SemaphoreType.DMA((5,)),
    ]
    return pl.pallas_call(
        functools.partial(weight_grad_kernel, micro_count),
        out_shape=jax.ShapeDtypeStruct((total_rows, width), bf),
        in_specs=[any_spec] * len(args),
        out_specs=any_spec,
        scratch_shapes=scratch,
        compiler_params=pltpu.CompilerParams(vmem_limit_bytes=VMEM_BYTES),
        cost_estimate=pl.CostEstimate(
            flops=2 * micro_count * rows * used * width,
            bytes_accessed=40_000_000,
            transcendentals=0,
        ),
    )(*args)


def ring_sum_kernel(
    chips,
    lanes,
    part_ref,
    sum_ref,
    held,
    from_core,
    arriving,
    final,
    load_sem,
    core_send,
    core_recv,
    ring_send,
    ring_recv,
    spread_send,
    spread_recv,
    cross_send,
    cross_recv,
    store_sem,
):
    line_len = chips // 2
    pipe = lax.axis_index("pipe")
    batch = lax.axis_index("batch")
    core = batch % 2
    side = (batch // 2) % 2
    line = batch // 4
    place = line * (1 - side) + (chips - 1 - line) * side

    def chip_at(spot):
        far = spot // line_len
        along = spot * (1 - far) + (chips - 1 - spot) * far
        return (pipe, (along * 2 + far) * 2 + core)

    onward = chip_at((place + 1) % chips)
    backward = chip_at((place + chips - 1) % chips)
    twin = (pipe, batch + 1 - 2 * core)

    barrier = pltpu.get_barrier_semaphore()
    for other in (onward, backward, twin):
        pl.semaphore_signal(barrier, inc=1, device_id=other, device_id_type=MESH_IDS)

    def chunk_of(rank):
        half_up = (rank + 1) // 2
        sign = 1 - 2 * (rank % 2)
        return (place + chips + sign * half_up) % chips

    def load(rank):
        chunk = chunk_of(rank)
        return pltpu.make_async_copy(part_ref.at[core, chunk], held.at[chunk], load_sem.at[rank])

    def swap(rank):
        chunk = chunk_of(rank)
        return pltpu.make_async_remote_copy(
            src_ref=part_ref.at[1 - core, chunk],
            dst_ref=from_core.at[chunk],
            send_sem=core_send.at[rank],
            recv_sem=core_recv.at[rank],
            device_id=twin,
            device_id_type=MESH_IDS,
        )

    for rank in range(chips):
        load(rank).start()
    pl.semaphore_wait(barrier, 3)
    for rank in range(chips):
        swap(rank).start()

    def add_rows(chunk, first, count, source):
        def one(index, carry):
            rows = pl.ds(pl.multiple_of(first + index * TILE, TILE), TILE)
            held[chunk, rows, :] = (
                held[chunk, rows, :].astype(jnp.float32) + source[rows, :].astype(jnp.float32)
            ).astype(jnp.bfloat16)
            return carry

        lax.fori_loop(0, count // TILE, one, 0, unroll=False)

    def prepare(rank):
        chunk = chunk_of(rank)
        load(rank).wait()
        swap(rank).wait_recv()
        add_rows(chunk, 0, held.shape[1], from_core.at[chunk])

    def ring_chunk(lane, step):
        return (place + (chips - 1) * chips - lanes[lane][0] * step) % chips

    def ring_copy(lane, step):
        sign, first, count = lanes[lane]
        chunk = ring_chunk(lane, step)
        rows = pl.ds(first, count)
        return pltpu.make_async_remote_copy(
            src_ref=held.at[chunk, rows],
            dst_ref=arriving.at[step, rows],
            send_sem=ring_send.at[lane, step],
            recv_sem=ring_recv.at[lane, step],
            device_id=onward if sign > 0 else backward,
            device_id_type=MESH_IDS,
        )

    def take(lane, step):
        sign, first, count = lanes[lane]
        chunk = ring_chunk(lane, step)
        ring_copy(lane, step - 1).wait_recv()
        add_rows(chunk, first, count, arriving.at[step - 1])

    prepare(0)
    for lane in range(len(lanes)):
        ring_copy(lane, 0).start()

    def early_step(step, carry):
        prepare(2 * step - 1)

        @pl.when(2 * step < chips)
        def _():
            prepare(2 * step)

        for lane in range(len(lanes)):
            take(lane, step)
            ring_copy(lane, step).start()
        return carry

    def late_step(step, carry):
        for lane in range(len(lanes)):
            take(lane, step)
            ring_copy(lane, step).start()
        return carry

    lax.fori_loop(1, chips // 2 + 1, early_step, 0)
    lax.fori_loop(chips // 2 + 1, chips - 1, late_step, 0)

    def spread_parts(lane, step):
        sign, first, count = lanes[lane]
        chunk = (place + (chips + 1) * chips + sign * (1 - step)) % chips
        return sign, chunk, pl.ds(first, count)

    def spread_copy(lane, step, source):
        sign, chunk, rows = spread_parts(lane, step)
        return pltpu.make_async_remote_copy(
            src_ref=source.at[chunk, rows],
            dst_ref=final.at[chunk, rows],
            send_sem=spread_send.at[lane, step],
            recv_sem=spread_recv.at[lane, step],
            device_id=onward if sign > 0 else backward,
            device_id_type=MESH_IDS,
        )

    def cross_copy(lane, step, source):
        sign, chunk, rows = spread_parts(lane, step)
        return pltpu.make_async_remote_copy(
            src_ref=source.at[chunk, rows],
            dst_ref=sum_ref.at[core, chunk, rows],
            send_sem=cross_send.at[lane, step],
            recv_sem=cross_recv.at[lane, step],
            device_id=twin,
            device_id_type=MESH_IDS,
        )

    def store_copy(lane, step, source):
        sign, chunk, rows = spread_parts(lane, step)
        return pltpu.make_async_copy(
            source.at[chunk, rows], sum_ref.at[core, chunk, rows], store_sem.at[lane, step]
        )

    for lane in range(len(lanes)):
        take(lane, chips - 1)
        spread_copy(lane, 0, held).start()
        cross_copy(lane, 0, held).start()
        store_copy(lane, 0, held).start()

    def spread_step(step, carry):
        for lane in range(len(lanes)):
            spread_copy(lane, step - 1, final).wait_recv()
            spread_copy(lane, step, final).start()
            cross_copy(lane, step, final).start()
            store_copy(lane, step, final).start()
        return carry

    lax.fori_loop(1, chips - 1, spread_step, 0)
    for lane in range(len(lanes)):
        spread_copy(lane, chips - 2, final).wait_recv()
        cross_copy(lane, chips - 1, final).start()
        store_copy(lane, chips - 1, final).start()

    def settle_swap(rank, carry):
        swap(rank).wait_send()
        return carry

    def settle_ring(step, carry):
        for lane in range(len(lanes)):
            ring_copy(lane, step).wait_send()
            spread_copy(lane, step, final).wait_send()
        return carry

    def settle_out(step, carry):
        for lane in range(len(lanes)):
            cross_copy(lane, step, final).wait()
            store_copy(lane, step, final).wait()
        return carry

    lax.fori_loop(0, chips, settle_swap, 0)
    lax.fori_loop(0, chips - 1, settle_ring, 0)
    lax.fori_loop(0, chips, settle_out, 0)


def ring_sum(parts, devices):
    total_rows, columns = parts.shape
    chips = devices // 2
    chunk_rows = total_rows // devices
    tiles = chunk_rows // TILE
    counts = [tiles // 4 + (1 if spot < tiles % 4 else 0) for spot in range(4)]
    lanes = []
    first = 0
    for sign, count in zip((1, -1, 1, -1), counts):
        lanes.append((sign, first * TILE, count * TILE))
        first += count
    block = (chips, chunk_rows, columns)
    dma = pltpu.SemaphoreType.DMA
    summed = pl.pallas_call(
        functools.partial(ring_sum_kernel, chips, tuple(lanes)),
        out_shape=jax.ShapeDtypeStruct((2,) + block, jnp.bfloat16),
        in_specs=[pl.BlockSpec(memory_space=pl.ANY)],
        out_specs=pl.BlockSpec(memory_space=pl.ANY),
        scratch_shapes=[
            pltpu.VMEM(block, jnp.bfloat16),
            pltpu.VMEM(block, jnp.bfloat16),
            pltpu.VMEM(block, jnp.bfloat16),
            pltpu.VMEM(block, jnp.bfloat16),
            dma((chips,)),
            dma((chips,)),
            dma((chips,)),
            dma((4, chips)),
            dma((4, chips)),
            dma((4, chips)),
            dma((4, chips)),
            dma((4, chips)),
            dma((4, chips)),
            dma((4, chips)),
        ],
        compiler_params=pltpu.CompilerParams(
            collective_id=0, has_side_effects=True, vmem_limit_bytes=56 * 1024 * 1024
        ),
    )(parts.reshape((2,) + block))
    return summed.reshape(total_rows, columns)


def widen_kernel(rows_ref, out_ref):
    out_ref[...] = rows_ref[...].astype(jnp.float32)


def widen(rows, first, shape):
    height, columns = shape
    width = rows.shape[1]
    size = width // 2
    steps = height // size
    return pl.pallas_call(
        widen_kernel,
        out_shape=jax.ShapeDtypeStruct(shape, jnp.float32),
        grid=(columns // width, steps),
        in_specs=[pl.BlockSpec((size, width), lambda j, i: (first // size + j * steps + i, 0))],
        out_specs=pl.BlockSpec((size, width), lambda j, i: (i, j)),
        cost_estimate=pl.CostEstimate(
            flops=0, bytes_accessed=6 * height * columns, transcendentals=0
        ),
    )(rows)


def passed_along(block, axis, distance):
    devices = range(lax.axis_size(axis))
    route = [(i - distance, i) for i in devices if i - distance in devices]
    return lax.ppermute(block, axis, route)


def shards(
    inputs,
    cotangent,
    lengths,
    assign,
    query_key_value,
    out_weight,
    up_weight,
    down_weight,
    model_gains,
    model_shifts,
    hidden_gains,
    hidden_shifts,
):
    pipe_rank = lax.axis_index("pipe")
    micro_count = inputs.shape[0]
    width = inputs.shape[2]
    hidden = up_weight.shape[2]
    slots = range(micro_count)
    owners = assign[:, None] == jnp.arange(micro_count, dtype=jnp.int32)[None, :]
    slot_len = jnp.sum(jnp.where(owners, lengths[:, None], 0), axis=0).astype(jnp.int32)
    length = [slot_len[slot : slot + 1] for slot in slots]
    weights = (
        query_key_value[0],
        out_weight[0],
        up_weight[0],
        down_weight[0],
        model_gains[0],
        model_shifts[0],
        jnp.concatenate([hidden_gains, 1.0 / hidden_gains], axis=0),
        hidden_shifts[0],
    )
    lower = (pipe_rank == 0).astype(jnp.int32)[None]
    upper = (pipe_rank == 1).astype(jnp.int32)[None]

    forward = [forward_call(lower, length[slot], inputs[slot], weights) for slot in slots]
    middle = [passed_along(forward[slot][0], "pipe", 1) for slot in slots]
    forward = [
        forward_call(upper, length[slot], middle[slot], weights, forward[slot]) for slot in slots
    ]
    kept = [dict(zip(FWD_STATE, forward[slot][1:])) for slot in slots]
    backward = [
        backward_call(
            upper, length[slot], cotangent[slot], middle[slot], weights, kept[slot], True
        )
        for slot in slots
    ]
    returned = [passed_along(backward[slot][0], "pipe", -1) for slot in slots]
    backward = [
        backward_call(
            lower, length[slot], returned[slot], inputs[slot], weights, kept[slot], False,
            backward[slot],
        )
        for slot in slots
    ]
    grads = [dict(zip(BWD_STATE, backward[slot][1:])) for slot in slots]
    devices = lax.axis_size("batch")
    rows = ring_sum(weight_grads(kept, grads, devices), devices)
    blocks = 4 + hidden // width
    ends = (blocks + hidden // width) * width
    vectors = rows[ends : ends + SUM_ROWS].astype(jnp.float32)
    wide = hidden // width
    return (
        jnp.stack([forward[slot][0] for slot in slots])[None],
        jnp.stack([backward[slot][0] for slot in slots])[None],
        widen(rows, 0, (width, 3 * width))[None],
        widen(rows, 3 * width, (width, width))[None],
        widen(rows, 4 * width, (width, hidden))[None],
        widen(rows, blocks * width, (hidden, width))[None],
        vectors[None, 0:3],
        vectors[None, 3:10],
        vectors[10 : 10 + wide].reshape(1, hidden),
        vectors[10 + wide : 10 + 3 * wide].reshape(1, 2, hidden),
    )


def solution(mesh):
    return jax.shard_map(
        shards,
        mesh=mesh,
        in_specs=(
            P(None, "batch", None),
            P(None, "batch", None),
            P("batch"),
            P("batch"),
            P("pipe", None, None),
            P("pipe", None, None),
            P("pipe", None, None),
            P("pipe", None, None),
            P("pipe", None, None),
            P("pipe", None, None),
            P("pipe", None),
            P("pipe", None, None),
        ),
        out_specs=(
            P("pipe", None, "batch", None),
            P("pipe", None, "batch", None),
            P("pipe", None, None),
            P("pipe", None, None),
            P("pipe", None, None),
            P("pipe", None, None),
            P("pipe", None, None),
            P("pipe", None, None),
            P("pipe", None),
            P("pipe", None, None),
        ),
        check_vma=False,
    )
```

time: 1360 us -> 444 us (0.33)
  waiting for transfers between devices: 423 us -> 49.7 us
  Pallas kernels: 0 us -> 365 us
  matrix products: 269 us -> 0 us
  other arithmetic: 251 us -> 5.57 us
  local copies, waits for them, and re-layouts: 221 us -> 13.2 us
  blocking collectives: 147 us -> 0 us
  between operations: 19.6 us -> 1.04 us
    pallas_call x0 -> x14, Pallas kernels: none -> 365 us  [the longest x1 150 us: ring_sum(): pl.pallas_call(functools.partial(ring_sum_kernel, chips, tuple(lanes)), o...]
    dot_general x57 -> x0, matrix products: 269 us -> none  [the longest x12 64.3 us: multiply_left_t(): lax.dot_general(left, right, (((0,), (0,)), ((), ())), preferred_element_...]
    reduce_scatter x4 -> x0, waiting for transfers between devices: 251 us -> none  [the longest x1 114 us: shards(): lax.psum_scatter(totals[2], 'batch', scatter_dimension=1, tiled=True)]
    all_gather x4 -> x0, waiting for transfers between devices: 140 us -> none  [the longest x1 42.8 us: shards(): lax.all_gather(shares[0].astype(jnp.bfloat16), 'batch', axis=1, tiled=True)]
    reduce_sum x50 -> x1, other arithmetic: 104 us -> 0.76 us  [shards(): jnp.sum(jnp.where(owners, lengths[:, None], 0), axis=0).astype(jnp.int32)]
    unnamed x2 -> x0, blocking collectives: 90.8 us -> none
    unnamed x682 -> x24, local copies, waits for them, and re-layouts: 74.6 us -> 8.03 us
    dynamic_update_slice x29 -> x0, other arithmetic: 63.3 us -> none  [put_slot(): lax.dynamic_update_index_in_dim(buffer, jnp.where(usable, new_value, prev...]
  transfers between devices with their start and end apart: 15 -> 4, of which waited for: 9 -> 2; matrix products, arithmetic and copies ran while one was open for 25% -> 0% of each run, Pallas kernels for 0% -> 24%
where the time goes in v1:
time: 444 us; the launch traced here: 440 us
  Pallas kernels  365 us (82%)
  waiting for transfers between devices  49.7 us (11%)
  local copies, waits for them, and re-layouts  13.2 us (3%)
  other arithmetic  5.57 us (1%)
  starting transfers between devices  5.26 us (1%)
    pallas_call x1, Pallas kernels, ring_sum(): pl.pallas_call(functools.partial(ring_sum_kernel, chips, tuple(lanes)), o...  150 us
    pallas_call x4, Pallas kernels, backward_call(): pl.pallas_call(functools.partial(backward_kernel, previous is not None, m...  94.3 us
    pallas_call x4, Pallas kernels, forward_call(): pl.pallas_call(functools.partial(forward_kernel, previous is not None), o...  73.5 us
    ppermute x4, waiting for transfers between devices, passed_along(): return lax.ppermute(block, axis, route)  49.7 us
    pallas_call x4, Pallas kernels, widen(): pl.pallas_call(widen_kernel, out_shape=jax.ShapeDtypeStruct(shape, jnp.fl...  24 us
    pallas_call x1, Pallas kernels, weight_grads(): pl.pallas_call(functools.partial(weight_grad_kernel, micro_count), out_sh...  23.4 us
  transfers between devices with their start and end apart: 4, of which 2 were waited for; matrix products, arithmetic and copies ran while one was open for 0% of the time, Pallas kernels for 24%

profile of v1, /device:TPU:0, one launch (start us, length us, event | category | flops | bytes accessed | tf_op | source)
XLA Modules:
  0.0 440.1 jit_solution(6663797595283829210)
XLA Ops:
  0.7 0.8 fusion
  1.4 0.6 fusion.1
  2.0 1.3 copy.66
  3.3 0.7 broadcast_divide_fusion
  4.1 1.3 pad_maximum_fusion.gh
  5.4 1.3 copy.65
  6.7 2.7 slice_bitcast_fusion.3
  9.4 27.5 %shard_map.195 = (bf16[512,768]{1,0:T(8,128)(2,1)}, bf16[512,768]{1,0:T(8,128)(2,1)}, bf16[512,2304]{1,0:T(8,128)(2,1)}, f32[128,512]{1,0:T(8,128)}, f32[512,768...) custom-call(s32[1]{0:T(128)} %bitcast.1.flag_ref, ...), custom_call_target="tpu_custom_call" | custom-call | flops 7247757312 | bytes 40000000 | tf_op jit(solution)/shard_map/pallas_call | solution.py:239
  36.9 1.3 collective-permute-start
  38.3 0.0 copy-start.6
  38.3 27.0 %shard_map.197 = (bf16[512,768]{1,0:T(8,128)(2,1)}, bf16[512,768]{1,0:T(8,128)(2,1)}, bf16[512,2304]{1,0:T(8,128)(2,1)}, f32[128,512]{1,0:T(8,128)}, f32[512,768...) custom-call(s32[1]{0:T(128)} %bitcast.1.flag_ref, ...), custom_call_target="tpu_custom_call" | custom-call | flops 7247757312 | bytes 40000000 | tf_op jit(solution)/shard_map/pallas_call | solution.py:239
  65.3 1.3 collective-permute-start.1
  66.6 0.0 copy-done.6
  66.6 1.2 slice_bitcast_fusion.1
  67.9 0.0 collective-permute-done.x_hbm
  67.9 0.0 copy-start.5
  67.9 0.9 copy-done.5
  68.8 12.7 %shard_map.196 = (bf16[512,768]{1,0:T(8,128)(2,1)}, bf16[512,768]{1,0:T(8,128)(2,1)}, bf16[512,2304]{1,0:T(8,128)(2,1)}, f32[128,512]{1,0:T(8,128)}, f32[512,768...) custom-call(s32[1]{0:T(128)} %bitcast.flag_ref, ...), custom_call_target="tpu_custom_call", output_to_operand_aliasing={{0}: (11, {}), {1}: (12, {}), {2}: (13, {}), {3}: (14, {}),... | custom-call | flops 7247757312 | bytes 40000000 | tf_op jit(solution)/shard_map/pallas_call | solution.py:239
  81.4 13.6 %shard_map.199 = (bf16[512,768]{1,0:T(8,128)(2,1)}, bf16[512,768]{1,0:T(8,128)(2,1)}, bf16[512,3072]{1,0:T(8,128)(2,1)}, bf16[512,768]{1,0:T(8,128)(2,1)}, bf16[512,2304]{1,0:T(8,128)(2,1)}, /*index=5*/f32[32,768]{1,0:T(8,128)}) custom-call(s32[1]{0:T(128)} %bitcast.flag_ref, s32[1]{0:T(128)} %get-tuple-element.170.length_ref, ...), custom_call_target="tpu_custom_call" | custom-call | flops 7247757312 | bytes 40000000 | tf_op jit(solution)/shard_map/pallas_call | solution.py:490
  95.1 1.3 collective-permute-start.2
  96.4 0.0 collective-permute-done.1.x_hbm
  96.4 0.0 copy-start.4
  96.4 0.9 copy-done.4
  97.2 6.4 %shard_map.198 = (bf16[512,768]{1,0:T(8,128)(2,1)}, bf16[512,768]{1,0:T(8,128)(2,1)}, bf16[512,2304]{1,0:T(8,128)(2,1)}, f32[128,512]{1,0:T(8,128)}, f32[512,768...) custom-call(s32[1]{0:T(128)} %bitcast.flag_ref, ...), custom_call_target="tpu_custom_call", output_to_operand_aliasing={{0}: (11, {}), {1}: (12, {}), {2}: (13, {}), {3}: (14, {}),... | custom-call | flops 7247757312 | bytes 40000000 | tf_op jit(solution)/shard_map/pallas_call | solution.py:239
  103.6 13.1 %shard_map.201 = (bf16[512,768]{1,0:T(8,128)(2,1)}, bf16[512,768]{1,0:T(8,128)(2,1)}, bf16[512,3072]{1,0:T(8,128)(2,1)}, bf16[512,768]{1,0:T(8,128)(2,1)}, bf16[512,2304]{1,0:T(8,128)(2,1)}, /*index=5*/f32[32,768]{1,0:T(8,128)}) custom-call(s32[1]{0:T(128)} %bitcast.flag_ref, s32[1]{0:T(128)} %get-tuple-element.171.length_ref, ...), custom_call_target="tpu_custom_call" | custom-call | flops 7247757312 | bytes 40000000 | tf_op jit(solution)/shard_map/pallas_call | solution.py:490
  116.8 1.3 collective-permute-start.3
  118.1 21.5 %collective-permute-done.2.dy_hbm = bf16[512,768]{1,0:T(8,128)(2,1)S(1)} collective-permute-done((bf16[512,768]{1,0:T(8,128)(2,1)}, bf16[512,768]{1,0:T(8,128)(2,1)S(1)}, u32[]{:S(2)}, u32[]{:S(2)}) %collective-permute-start.2) | collective-permute-done | bytes 786464 | tf_op jit(solution)/shard_map/ppermute | solution.py:891
  139.6 0.9 copy-done.7
  140.4 33.7 %shard_map.200 = (bf16[512,768]{1,0:T(8,128)(2,1)}, bf16[512,768]{1,0:T(8,128)(2,1)}, bf16[512,3072]{1,0:T(8,128)(2,1)}, bf16[512,768]{1,0:T(8,128)(2,1)}, bf16[512,2304]{1,0:T(8,128)(2,1)}, /*index=5*/f32[32,768]{1,0:T(8,128)}) custom-call(s32[1]{0:T(128)} %bitcast.1.flag_ref, ...), custom_call_target="tpu_custom_call", output_to_operand_aliasing={{0}: (19, {}), {1}: (20, {}), {2}: (21, {}), {3}: (22, {}),... | custom-call | flops 7247757312 | bytes 40000000 | tf_op jit(solution)/shard_map/pallas_call | solution.py:490
  174.2 28.3 %collective-permute-done.3.dy_hbm = bf16[512,768]{1,0:T(8,128)(2,1)S(1)} collective-permute-done((bf16[512,768]{1,0:T(8,128)(2,1)}, bf16[512,768]{1,0:T(8,128)(2,1)S(1)}, u32[]{:S(2)}, u32[]{:S(2)}) %collective-permute-start.3) | collective-permute-done | bytes 786464 | tf_op jit(solution)/shard_map/ppermute | solution.py:891
  202.4 0.9 copy-done.8
  203.3 33.8 %shard_map.202 = (bf16[512,768]{1,0:T(8,128)(2,1)}, bf16[512,768]{1,0:T(8,128)(2,1)}, bf16[512,3072]{1,0:T(8,128)(2,1)}, bf16[512,768]{1,0:T(8,128)(2,1)}, bf16[512,2304]{1,0:T(8,128)(2,1)}, /*index=5*/f32[32,768]{1,0:T(8,128)}) custom-call(s32[1]{0:T(128)} %bitcast.1.flag_ref, ...), custom_call_target="tpu_custom_call", output_to_operand_aliasing={{0}: (19, {}), {1}: (20, {}), {2}: (21, {}), {3}: (22, {}),... | custom-call | flops 7247757312 | bytes 40000000 | tf_op jit(solution)/shard_map/pallas_call | solution.py:490
  237.2 23.4 %shard_map.203 = bf16[9472,768]{1,0:T(8,128)(2,1)} custom-call(bf16[512,3072]{1,0:T(8,128)(2,1)} %get-tuple-element.106.normed_hidden_hbm.refs_0_, bf16[512,768]{1,0:T(8,128)(2,1)} %get-tuple-element.130.refs_1_, bf16[512,768]{1,0:T(8,128)(2,1)} %get-tuple-element.131.refs_2_, bf16[512,768]{1,0:T(8,128)(2,1)} %get-tuple-element.132.refs_3_, ...), custom_call_target="tpu_custom_call" | custom-call | flops 14545846272 | bytes 40000000 | tf_op jit(solution)/shard_map/pallas_call | solution.py:607
  260.6 150.0 %shard_map.204 = bf16[2,8,592,768]{3,2,1,0:T(8,128)(2,1)} custom-call(bf16[2,8,592,768]{3,2,1,0:T(8,128)(2,1)} %bitcast.80), custom_call_target="tpu_custom_call" | custom-call | tf_op jit(solution)/shard_map/pallas_call | solution.py:839
  410.6 0.8 slice_convert_fusion
  411.5 2.6 shard_map.206
  414.0 6.0 %shard_map.205 = f32[768,2304]{1,0:T(8,128)} custom-call(bf16[9472,768]{1,0:T(8,128)(2,1)} %bitcast.45), custom_call_target="tpu_custom_call" | custom-call | bytes 10616832 | tf_op jit(solution)/shard_map/pallas_call | solution.py:876
  420.0 7.6 %shard_map.208 = f32[3072,768]{1,0:T(8,128)} custom-call(bf16[9472,768]{1,0:T(8,128)(2,1)} %bitcast.46), custom_call_target="tpu_custom_call" | custom-call | bytes 14155776 | tf_op jit(solution)/shard_map/pallas_call | solution.py:876
  427.7 7.8 %shard_map.207 = f32[768,3072]{1,0:T(8,128)} custom-call(bf16[9472,768]{1,0:T(8,128)(2,1)} %bitcast.47), custom_call_target="tpu_custom_call" | custom-call | bytes 14155776 | tf_op jit(solution)/shard_map/pallas_call | solution.py:876
  435.5 0.6 copy.62
  436.1 0.6 copy.58
  436.7 0.6 copy.59
  437.3 0.6 reshape.37
  438.0 0.0 copy-done
  438.0 0.0 copy-done.1
  438.0 0.0 copy-done.2
  438.0 0.0 copy-done.3
  438.0 1.9 maximum_bitcast_fusion
  (10 shorter events, 0.0 us)
Async XLA Ops:
  36.9 30.9 %collective-permute-start = (bf16[512,768]{1,0:T(8,128)(2,1)}, bf16[512,768]{1,0:T(8,128)(2,1)S(1)}, u32[]{:S(2)}, u32[]{:S(2)}) collective-permute-start(bf16[512,768]{1,0:T(8,128)(2,1)} %get-tuple-element.78.refs_0_), channel_id=1, source_target_pairs={{0,16},{1,17},{2,18},{3,19},{4,20},{5,21},{6,22},{7,23},{8,24},{9,... | collective-permute-start | bytes 2359304 | tf_op jit(solution)/shard_map/ppermute | solution.py:891
  38.3 28.3 %copy-start.6 = (bf16[2,512,768]{2,1,0:T(8,128)(2,1)S(1)}, bf16[2,512,768]{2,1,0:T(8,128)(2,1)}, u32[]{:S(2)}) copy-start(bf16[2,512,768]{2,1,0:T(8,128)(2,1)} %param.13) | copy-start | bytes 4718596
  65.3 31.1 %collective-permute-start.1 = (bf16[512,768]{1,0:T(8,128)(2,1)}, bf16[512,768]{1,0:T(8,128)(2,1)S(1)}, u32[]{:S(2)}, u32[]{:S(2)}) collective-permute-start(bf16[512,768]{1,0:T(8,128)(2,1)} %get-tuple-element.90.refs_0_), channel_id=1, source_target_pairs={{0,16},{1,17},{2,18},{3,19},{4,20},{5,21},{6,22},{7,23},{8,24},{9,... | collective-permute-start | bytes 2359304 | tf_op jit(solution)/shard_map/ppermute | solution.py:891
  67.9 0.9 copy-start.5
  95.1 44.5 %collective-permute-start.2 = (bf16[512,768]{1,0:T(8,128)(2,1)}, bf16[512,768]{1,0:T(8,128)(2,1)S(1)}, u32[]{:S(2)}, u32[]{:S(2)}) collective-permute-start(bf16[512,768]{1,0:T(8,128)(2,1)} %get-tuple-element.109.refs_0_), channel_id=1, source_target_pairs={{16,0},{17,1},{18,2},{19,3},{20,4},{21,5},{22,6},{23,7},{24,8},{25... | collective-permute-start | bytes 2359304 | tf_op jit(solution)/shard_map/ppermute | solution.py:891
  96.4 0.9 copy-start.4
  116.8 85.6 %collective-permute-start.3 = (bf16[512,768]{1,0:T(8,128)(2,1)}, bf16[512,768]{1,0:T(8,128)(2,1)S(1)}, u32[]{:S(2)}, u32[]{:S(2)}) collective-permute-start(bf16[512,768]{1,0:T(8,128)(2,1)} %get-tuple-element.123.refs_0_), channel_id=1, source_target_pairs={{16,0},{17,1},{18,2},{19,3},{20,4},{21,5},{22,6},{23,7},{24,8},{25... | collective-permute-start | bytes 2359304 | tf_op jit(solution)/shard_map/ppermute | solution.py:891
  139.6 0.9 copy-start.7
  202.4 0.9 copy-start.8
  427.7 10.3 %copy-start = (bf16[512,768]{1,0:T(8,128)(2,1)S(1)}, bf16[512,768]{1,0:T(8,128)(2,1)}, u32[]{:S(2)}) copy-start(bf16[512,768]{1,0:T(8,128)(2,1)} %get-tuple-element.101) | copy-start | bytes 2359300
  427.7 10.3 %copy-start.1 = (bf16[512,768]{1,0:T(8,128)(2,1)S(1)}, bf16[512,768]{1,0:T(8,128)(2,1)}, u32[]{:S(2)}) copy-start(bf16[512,768]{1,0:T(8,128)(2,1)} %get-tuple-element.115) | copy-start | bytes 2359300
  427.7 10.3 %copy-start.2 = (bf16[512,768]{1,0:T(8,128)(2,1)S(1)}, bf16[512,768]{1,0:T(8,128)(2,1)}, u32[]{:S(2)}) copy-start(bf16[512,768]{1,0:T(8,128)(2,1)} %get-tuple-element.129) | copy-start | bytes 2359300
  427.7 10.3 %copy-start.3 = (bf16[512,768]{1,0:T(8,128)(2,1)S(1)}, bf16[512,768]{1,0:T(8,128)(2,1)}, u32[]{:S(2)}) copy-start(bf16[512,768]{1,0:T(8,128)(2,1)} %get-tuple-element.89) | copy-start | bytes 2359300
